TPU v7x, 32 devices: a whole 2x2x4 slice. The times are simulated.
32 devices in a mesh: dp: 8 (over z, y), fsdp: 4 (over x, core).
Axes of the slice: x: 2, y: 2, z: 4, core: 2. Of those that a mesh axis runs over, the one named last changes fastest.
Arguments:
- tokens: bfloat16 [8192, 768], P(('dp', 'fsdp')), may hold values from -6 to 6
- segment: int32 [8192], P(('dp', 'fsdp')), may hold values from 0 to 3, as said below
- buckets: int32 [2047], replicated, may hold values from 0 to 31
- routes: int32 [8192, 1], P(('dp', 'fsdp')), may hold values from 0 to 3; in each aligned block of 256 rows (0 to 255, 256 to 511, ...) at most 128 rows name the same one
- w_query: bfloat16 [768, 768], P(('dp', 'fsdp')), may hold values from -0.0546875 to 0.0546875
- w_key: bfloat16 [768, 768], P(('dp', 'fsdp')), may hold values from -0.21875 to 0.21875
- w_value: bfloat16 [768, 768], P(('dp', 'fsdp')), may hold values from -0.21875 to 0.21875
- w_output: bfloat16 [768, 768], P(('dp', 'fsdp')), may hold values from -1.75 to 1.75
- w_router: bfloat16 [768, 4], P(('dp', 'fsdp')), may hold values from -0.15625 to 0.15625
- norm_attn: bfloat16 [768], P(('dp', 'fsdp')), may hold values from 0.5 to 1.5
- norm_ffn: bfloat16 [768], P(('dp', 'fsdp')), may hold values from 0.5 to 1.5
- bias_table: bfloat16 [32, 12], replicated, may hold values from -4 to 4
- expert_in: bfloat16 [4, 768, 3072], P('fsdp', None, 'dp'), may hold values from -0.21875 to 0.21875
- expert_out: bfloat16 [4, 3072, 768], P('fsdp', 'dp'), may hold values from -0.75 to 0.75
- out_grad: bfloat16 [8192, 768], P(('dp', 'fsdp')), may hold values from -6 to 6
Outputs:
- mixed: bfloat16 [8192, 768], P(('dp', 'fsdp'))
- d_tokens: bfloat16 [8192, 768], P(('dp', 'fsdp'))
- d_w_query: float32 [768, 768], P(('dp', 'fsdp'))
- d_w_key: float32 [768, 768], P(('dp', 'fsdp'))
- d_w_value: float32 [768, 768], P(('dp', 'fsdp'))
- d_w_output: float32 [768, 768], P(('dp', 'fsdp'))
- d_w_router: float32 [768, 4], P(('dp', 'fsdp'))
- d_norm_attn: float32 [768], P(('dp', 'fsdp'))
- d_norm_ffn: float32 [768], P(('dp', 'fsdp'))
- d_bias_table: float32 [32, 12], replicated
- d_expert_in: float32 [4, 768, 3072], P('fsdp', None, 'dp')
- d_expert_out: float32 [4, 3072, 768], P('fsdp', 'dp')
Inputs may be any that keep to these rules, and one draw needn't show every extreme that they name: `segment`: within each group of 1024 consecutive tokens the ids never fall and start at 0; each id 0 to 3 holds at least one token of each group. `routes`: at most 128 of the rows of one device name the same expert.
All inputs are finite; a program needn't handle non-finite values.
Results may differ from a plain program's by a relative error of at most 0.02.
Values may be sent and summed in bfloat16 or wider, within the bound.
No kernel may reach another device: no remote copies, remote signals or barrier semaphores. Data moves between devices by JAX's collectives and lax.ppermute only.
A program may use at most 128 MiB of HBM per device.

v0:
```python
import math

import jax
import jax.numpy as jnp
from jax import lax
from jax.sharding import PartitionSpec as P

HEADS = 12
HEAD = 64
BUCKETS = 32


EPSILON = 1e-06
MASKED = -1000000000.0
HIGHEST = lax.Precision.HIGHEST


def normalize(values, scale):
    return values * lax.rsqrt(jnp.mean(values * values, axis=-1, keepdims=True) + EPSILON) * scale


def gelu_tanh(values):
    return jax.nn.gelu(values, approximate=True)


def choose_gate(logits, picked_float):
    return jnp.sum(jax.nn.softmax(logits, axis=-1) * picked_float, axis=-1)


def product(left, right):
    return jnp.dot(left, right, preferred_element_type=jnp.float32)


def contract_rows(left, right, precision=None):
    return lax.dot_general(
        left,
        right,
        (((0,), (0,)), ((), ())),
        precision=precision,
        preferred_element_type=jnp.float32,
    )


def contract_cols(left, right):
    return lax.dot_general(
        left, right, (((1,), (1,)), ((), ())), preferred_element_type=jnp.float32
    )


def bucket_onehot(buckets, query_places, key_places, group_rows):
    index = key_places[None, :] - query_places[:, None] + (group_rows - 1)
    ids = jnp.take(buckets, index, axis=0)
    return (jnp.arange(BUCKETS, dtype=jnp.int32)[:, None, None] == ids[None, :, :]).astype(
        jnp.bfloat16
    )


def bias_from(bias_lookup, one_hot_matrix):
    return jnp.einsum(
        "ne,nzg->ezg", bias_lookup, one_hot_matrix, preferred_element_type=jnp.float32
    )


def table_from(score_gradient, one_hot_matrix):
    return jnp.einsum(
        "plf,jlf->jp", score_gradient, one_hot_matrix, preferred_element_type=jnp.float32
    )


def scored(query_heads, key_heads, bias_tile, keep):
    scores = jnp.einsum("qhe,khe->hqk", query_heads, key_heads, preferred_element_type=jnp.float32)
    return jnp.where(keep[None], scores + bias_tile, MASKED)


def body(
    tokens,
    segment,
    buckets,
    routes,
    w_query,
    w_key,
    w_value,
    w_output,
    w_router,
    norm_attn,
    norm_ffn,
    bias_table,
    expert_in,
    expert_out,
    out_grad,
):
    tok_rows, model_width = tokens.shape
    expert_count = lax.axis_size("fsdp")
    group_rows = tok_rows * expert_count
    capacity = 2 * tok_rows // expert_count
    gathered = (
        lax.all_gather(w_query, ("dp", "fsdp"), axis=0, tiled=True),
        lax.all_gather(w_key, ("dp", "fsdp"), axis=0, tiled=True),
        lax.all_gather(w_value, ("dp", "fsdp"), axis=0, tiled=True),
        lax.all_gather(w_output, ("dp", "fsdp"), axis=0, tiled=True),
        lax.all_gather(w_router, ("dp", "fsdp"), axis=0, tiled=True),
        lax.all_gather(norm_attn, ("dp", "fsdp"), axis=0, tiled=True),
        lax.all_gather(norm_ffn, ("dp", "fsdp"), axis=0, tiled=True),
    )
    weight_query, weight_key, weight_value, weight_output, weight_router, gain_attn, gain_ffn = (
        gathered
    )
    gain_attn = gain_attn.astype(jnp.float32)
    gain_ffn = gain_ffn.astype(jnp.float32)
    whole_in, whole_out = (
        lax.all_gather(expert_in, "dp", axis=2, tiled=True),
        lax.all_gather(expert_out, "dp", axis=1, tiled=True),
    )
    weight_in = whole_in[0]
    weight_out = whole_out[0]
    inputs = tokens.astype(jnp.float32)
    normed, norm_back = jax.vjp(normalize, inputs, gain_attn)
    hidden = normed.astype(jnp.bfloat16)
    queries = product(hidden, weight_query).astype(jnp.bfloat16)
    keys = product(hidden, weight_key).astype(jnp.bfloat16)
    values = product(hidden, weight_value).astype(jnp.bfloat16)
    query_heads = queries.reshape(tok_rows, HEADS, HEAD)
    key_heads = keys.reshape(tok_rows, HEADS, HEAD)
    head_values = values.reshape(tok_rows, HEADS, HEAD)
    first_query = lax.axis_index("fsdp") * tok_rows
    query_places = first_query + jnp.arange(tok_rows, dtype=jnp.int32)

    def key_block(piece, offset, block_rows):
        key_piece, value_piece, seg_piece = piece
        key_portion = lax.dynamic_slice_in_dim(key_piece, offset, block_rows, 0).reshape(
            block_rows, HEADS, HEAD
        )
        value_part = lax.dynamic_slice_in_dim(value_piece, offset, block_rows, 0).reshape(
            block_rows, HEADS, HEAD
        )
        seg_part = lax.dynamic_slice_in_dim(seg_piece, offset, block_rows, 0)
        key_places = offset + jnp.arange(block_rows, dtype=jnp.int32)
        one_hot_matrix = bucket_onehot(buckets, query_places, key_places, group_rows)
        keep = segment[:, None] == seg_part[None, :]
        return (key_portion, value_part, one_hot_matrix, keep)

    initial_state = (
        jnp.full((HEADS, tok_rows), 2.0 * MASKED, jnp.float32),
        jnp.zeros((HEADS, tok_rows), jnp.float32),
        jnp.zeros((tok_rows, HEADS, HEAD), jnp.float32),
    )
    piece = (
        lax.all_gather(keys, "fsdp", axis=0, tiled=True),
        lax.all_gather(values, "fsdp", axis=0, tiled=True),
        lax.all_gather(segment, "fsdp", axis=0, tiled=True),
    )
    piece_rows = piece[0].shape[0]
    block_rows = math.gcd(piece_rows, 512)

    def attend_visit(turn, state):
        running_max, running_sum, running_acc = state
        key_portion, value_part, one_hot_matrix, keep = key_block(
            piece, turn * block_rows, block_rows
        )
        scores = scored(query_heads, key_portion, bias_from(bias_table, one_hot_matrix), keep)
        new_max = jnp.maximum(running_max, jnp.max(scores, axis=-1))
        shrink = jnp.exp(running_max - new_max)
        weights = jnp.exp(scores - new_max[..., None])
        running_sum = running_sum * shrink + jnp.sum(weights, axis=-1)
        running_acc = running_acc * shrink.T[:, :, None] + jnp.einsum(
            "hqk,khe->qhe",
            weights.astype(jnp.bfloat16),
            value_part,
            preferred_element_type=jnp.float32,
        )
        return (new_max, running_sum, running_acc)

    top_score, total_weight, summed = lax.fori_loop(
        0, piece_rows // block_rows, attend_visit, initial_state
    )
    log_total = top_score + jnp.log(total_weight)
    attn_out = (
        (summed / total_weight.T[:, :, None]).reshape(tok_rows, model_width).astype(jnp.bfloat16)
    )
    residual = inputs + product(attn_out, weight_output)
    normalized_second2, norm_back2 = jax.vjp(normalize, residual, gain_ffn)
    hidden2 = normalized_second2.astype(jnp.bfloat16)
    logits = product(hidden2, weight_router)
    route = routes[:, 0]
    picked = (route[:, None] == jnp.arange(expert_count, dtype=jnp.int32)[None, :]).astype(
        jnp.int32
    )
    picked_float = picked.astype(jnp.float32)
    gate, gate_back = jax.vjp(lambda logit_rows: choose_gate(logit_rows, picked_float), logits)
    rank = jnp.sum((jnp.cumsum(picked, axis=0) - 1) * picked, axis=1)
    slot = route * capacity + rank
    placing = (
        jnp.arange(expert_count * capacity, dtype=jnp.int32)[:, None] == slot[None, :]
    ).astype(jnp.bfloat16)
    outgoing = (
        product(placing, hidden2).astype(jnp.bfloat16).reshape(expert_count, capacity, model_width)
    )
    arrived = lax.all_to_all(outgoing, "fsdp", split_axis=0, concat_axis=0, tiled=True).reshape(
        expert_count * capacity, model_width
    )
    pre_act = product(arrived, weight_in)
    activated = gelu_tanh(pre_act).astype(jnp.bfloat16)
    expert_result = (
        product(activated, weight_out)
        .astype(jnp.bfloat16)
        .reshape(expert_count, capacity, model_width)
    )
    returned = lax.all_to_all(
        expert_result, "fsdp", split_axis=0, concat_axis=0, tiled=True
    ).reshape(expert_count * capacity, model_width)
    token_result = contract_rows(placing, returned)
    mixed = residual + gate[:, None] * token_result
    grad_out = out_grad.astype(jnp.float32)
    d_gate = jnp.sum(grad_out * token_result, axis=-1)
    d_logits = gate_back(d_gate)[0].astype(jnp.bfloat16)
    d_router = contract_rows(hidden2, d_logits)
    d_token_result = (gate[:, None] * grad_out).astype(jnp.bfloat16)
    d_outgoing = (
        product(placing, d_token_result)
        .astype(jnp.bfloat16)
        .reshape(expert_count, capacity, model_width)
    )
    d_arrived = lax.all_to_all(d_outgoing, "fsdp", split_axis=0, concat_axis=0, tiled=True).reshape(
        expert_count * capacity, model_width
    )
    d_activated = contract_cols(d_arrived, weight_out)
    gelu_value, gelu_back = jax.vjp(gelu_tanh, pre_act)
    d_pre_act = gelu_back(d_activated)[0].astype(jnp.bfloat16)
    d_weight_out = contract_rows(activated, d_arrived)
    d_weight_in = contract_rows(arrived, d_pre_act)
    d_rows_in = contract_cols(d_pre_act, weight_in)
    d_back = (
        lax.all_to_all(
            d_rows_in.reshape(expert_count, capacity, model_width).astype(jnp.bfloat16),
            "fsdp",
            split_axis=0,
            concat_axis=0,
            tiled=True,
        )
        .astype(jnp.float32)
        .reshape(expert_count * capacity, model_width)
    )
    d_hidden2 = contract_rows(placing.astype(jnp.float32), d_back, HIGHEST) + contract_cols(
        d_logits, weight_router
    )
    d_residual_norm, d_gain_ffn = norm_back2(d_hidden2)
    residual_gradient = grad_out + d_residual_norm
    d_branch = residual_gradient.astype(jnp.bfloat16)
    d_weight_output = contract_rows(attn_out, d_branch)
    d_attended = contract_cols(d_branch, weight_output).astype(jnp.bfloat16)
    d_out_heads = d_attended.reshape(tok_rows, HEADS, HEAD)
    correction = jnp.einsum(
        "qhe,qhe->hq",
        d_out_heads.astype(jnp.float32),
        attn_out.reshape(tok_rows, HEADS, HEAD).astype(jnp.float32),
    )

    def block_grads(piece, offset, block_rows):
        key_portion, value_part, one_hot_matrix, keep = key_block(piece, offset, block_rows)
        probs = jnp.exp(
            scored(query_heads, key_portion, bias_from(bias_table, one_hot_matrix), keep)
            - log_total[..., None]
        )
        grad_probs = jnp.einsum(
            "qhe,khe->hqk", d_out_heads, value_part, preferred_element_type=jnp.float32
        )
        score_gradient = (probs * (grad_probs - correction[..., None])).astype(jnp.bfloat16)
        return (key_portion, probs, score_gradient, table_from(score_gradient, one_hot_matrix))

    def key_side(carry, piece):
        piece_rows = piece[0].shape[0]
        block_rows = math.gcd(piece_rows, 512)

        def key_visit(turn, state):
            grad_query, grad_table = state
            key_portion, probs, score_gradient, table_term = block_grads(
                piece, turn * block_rows, block_rows
            )
            grad_query = grad_query + jnp.einsum(
                "hqk,khe->qhe", score_gradient, key_portion, preferred_element_type=jnp.float32
            )
            return (grad_query, grad_table + table_term)

        return lax.fori_loop(0, piece_rows // block_rows, key_visit, carry)

    key_state = (
        jnp.zeros((tok_rows, HEADS, HEAD), jnp.float32),
        jnp.zeros((BUCKETS, HEADS), jnp.float32),
    )
    folded = key_side(
        key_state,
        (
            lax.all_gather(keys, "fsdp", axis=0, tiled=True),
            lax.all_gather(values, "fsdp", axis=0, tiled=True),
            lax.all_gather(segment, "fsdp", axis=0, tiled=True),
        ),
    )
    grad_query_heads, table_local = folded
    all_log, all_correction, all_seg = (
        lax.all_gather(log_total.T, "fsdp", axis=0, tiled=True),
        lax.all_gather(correction.T, "fsdp", axis=0, tiled=True),
        lax.all_gather(segment.astype(jnp.float32), "fsdp", axis=0, tiled=True),
    )
    query_state = (
        jnp.zeros((tok_rows, HEADS, HEAD), jnp.float32),
        jnp.zeros((tok_rows, HEADS, HEAD), jnp.float32),
    )
    query_piece = lax.all_gather(queries, "fsdp", axis=0, tiled=True)
    grad_piece = lax.all_gather(d_attended, "fsdp", axis=0, tiled=True)
    piece_rows = query_piece.shape[0]
    query_block_rows = math.gcd(piece_rows, 512)

    def query_visit(turn, state):
        grad_keys, grad_values = state
        offset = turn * query_block_rows
        query_part = lax.dynamic_slice_in_dim(query_piece, offset, query_block_rows, 0).reshape(
            query_block_rows, HEADS, HEAD
        )
        grad_part = lax.dynamic_slice_in_dim(grad_piece, offset, query_block_rows, 0).reshape(
            query_block_rows, HEADS, HEAD
        )
        log_part = lax.dynamic_slice_in_dim(all_log, offset, query_block_rows, 0).T
        correction_part = lax.dynamic_slice_in_dim(all_correction, offset, query_block_rows, 0).T
        seg_part = lax.dynamic_slice_in_dim(all_seg, offset, query_block_rows, 0).astype(jnp.int32)
        row_places = offset + jnp.arange(query_block_rows, dtype=jnp.int32)
        one_hot_matrix = bucket_onehot(buckets, row_places, query_places, group_rows)
        keep = seg_part[:, None] == segment[None, :]
        probs = jnp.exp(
            scored(query_part, key_heads, bias_from(bias_table, one_hot_matrix), keep)
            - log_part[..., None]
        )
        grad_probs = jnp.einsum(
            "qhe,khe->hqk", grad_part, head_values, preferred_element_type=jnp.float32
        )
        score_gradient = (probs * (grad_probs - correction_part[..., None])).astype(jnp.bfloat16)
        grad_keys = grad_keys + jnp.einsum(
            "hqk,qhe->khe", score_gradient, query_part, preferred_element_type=jnp.float32
        )
        grad_values = grad_values + jnp.einsum(
            "hqk,qhe->khe",
            probs.astype(jnp.bfloat16),
            grad_part,
            preferred_element_type=jnp.float32,
        )
        return (grad_keys, grad_values)

    grad_key_heads, grad_value_heads = lax.fori_loop(
        0, piece_rows // query_block_rows, query_visit, query_state
    )
    grad_key_rows = grad_key_heads.reshape(tok_rows, model_width)
    grad_value_rows = grad_value_heads.reshape(tok_rows, model_width)
    d_queries = grad_query_heads.reshape(tok_rows, model_width).astype(jnp.bfloat16)
    d_keys = grad_key_rows.astype(jnp.bfloat16)
    d_values = grad_value_rows.astype(jnp.bfloat16)
    d_weight_query = contract_rows(hidden, d_queries)
    d_weight_key = contract_rows(hidden, d_keys)
    d_weight_value = contract_rows(hidden, d_values)
    d_hidden = (
        contract_cols(d_queries, weight_query)
        + contract_cols(d_keys, weight_key)
        + contract_cols(d_values, weight_value)
    )
    d_inputs_norm, d_gain_attn = norm_back(d_hidden)
    d_inputs = (residual_gradient + d_inputs_norm).astype(jnp.bfloat16)
    dense_parts = (
        lax.psum_scatter(d_weight_query, ("dp", "fsdp"), scatter_dimension=0, tiled=True),
        lax.psum_scatter(d_weight_key, ("dp", "fsdp"), scatter_dimension=0, tiled=True),
        lax.psum_scatter(d_weight_value, ("dp", "fsdp"), scatter_dimension=0, tiled=True),
        lax.psum_scatter(d_weight_output, ("dp", "fsdp"), scatter_dimension=0, tiled=True),
        lax.psum_scatter(d_router, ("dp", "fsdp"), scatter_dimension=0, tiled=True),
        lax.psum_scatter(d_gain_attn, ("dp", "fsdp"), scatter_dimension=0, tiled=True),
        lax.psum_scatter(d_gain_ffn, ("dp", "fsdp"), scatter_dimension=0, tiled=True),
    )
    expert_parts = (
        lax.psum_scatter(
            d_weight_in[None].astype(jnp.bfloat16), "dp", scatter_dimension=2, tiled=True
        ).astype(jnp.float32),
        lax.psum_scatter(
            d_weight_out[None].astype(jnp.bfloat16), "dp", scatter_dimension=1, tiled=True
        ).astype(jnp.float32),
    )
    table_total = lax.psum(table_local, ("dp", "fsdp"))
    return (
        mixed.astype(jnp.bfloat16),
        d_inputs,
        dense_parts[0],
        dense_parts[1],
        dense_parts[2],
        dense_parts[3],
        dense_parts[4],
        dense_parts[5],
        dense_parts[6],
        table_total,
        expert_parts[0],
        expert_parts[1],
    )


def solution(mesh):
    return jax.shard_map(
        body,
        mesh=mesh,
        in_specs=(
            P(("dp", "fsdp"), None),
            P(("dp", "fsdp")),
            P(),
            P(("dp", "fsdp"), None),
            P(("dp", "fsdp"), None),
            P(("dp", "fsdp"), None),
            P(("dp", "fsdp"), None),
            P(("dp", "fsdp"), None),
            P(("dp", "fsdp"), None),
            P(("dp", "fsdp")),
            P(("dp", "fsdp")),
            P(),
            P("fsdp", None, "dp"),
            P("fsdp", "dp", None),
            P(("dp", "fsdp"), None),
        ),
        out_specs=(
            P(("dp", "fsdp"), None),
            P(("dp", "fsdp"), None),
            P(("dp", "fsdp"), None),
            P(("dp", "fsdp"), None),
            P(("dp", "fsdp"), None),
            P(("dp", "fsdp"), None),
            P(("dp", "fsdp"), None),
            P(("dp", "fsdp")),
            P(("dp", "fsdp")),
            P(),
            P("fsdp", None, "dp"),
            P("fsdp", "dp", None),
        ),
        check_vma=False,
    )
```

profile of v0, /device:TPU:0, one launch (start us, length us, event | category | flops | bytes accessed | tf_op | source)
XLA Modules:
  0.0 6249.5 jit_solution(5128404611193924940)
XLA Ops:
  11.2 42.0 all-reduce.6
  54.4 13.4 all-gather.20.cloned.1.call-done
  67.8 2.7 convolution_convert_fusion.5
  70.6 53.1 all-gather.14.cloned.1.call-done
  123.7 2.7 convolution_convert_fusion.7
  129.1 5.2 all-gather
  136.6 43.1 all-gather.18.cloned.1.call-done
  182.4 17.3 all-gather.22.cloned.1.call-done
  199.7 2.6 copy.77
  202.3 19.1 all-gather.16.cloned.1.call-done
  221.4 2.6 copy.76
  224.0 1500.0 %while.52 = (s32[]{:T(128)}, f32[12,256]{1,0:T(8,128)}, f32[12,256]{1,0:T(8,128)}, f32[256,12,64]{0,2,1:T(8,128)}, s32[256]{0:T(256)S(1)}, /*index=5*/s32[1024]{...) while((s32[]{:T(128)}, f32[12,256]{1,0:T(8,128)}, ...), condition=%wide.region_4.6_spmd.clone, body=%wide.region_1.5_spmd.clone.sunk | while | flops 521227008 | bytes 72909240 | solution.py:173
  225.4 724.9 %gather_fusion = s32[131072]{0:T(1024)S(1)} fusion(s32[2047]{0:T(1024)S(1)} %get-tuple-element.1461, s32[131072]{0:T(1024)S(1)} %broadcast_clamp_fusion.6), kind=kCustom, calls=%fused_computation.clone.clone.1 | custom fusion | bytes 1572864 | tf_op jit(solution)/shard_map/while/body/eval_jaxpr/jit(_take)/gather | solution.py:52
  951.9 5.9 fusion.235
  957.8 9.2 copy.132
  967.0 4.1 fusion.236
  975.4 724.9 %gather_fusion = s32[131072]{0:T(1024)S(1)} fusion(s32[2047]{0:T(1024)S(1)} %get-tuple-element.1461, s32[131072]{0:T(1024)S(1)} %broadcast_clamp_fusion.6), kind=kCustom, calls=%fused_computation.clone.clone.1 | custom fusion | bytes 1572864 | tf_op jit(solution)/shard_map/while/body/eval_jaxpr/jit(_take)/gather | solution.py:52
  1701.9 5.9 fusion.235
  1707.8 9.2 copy.132
  1717.0 4.1 fusion.236
  1729.1 14.3 all_to_all.20
  1743.4 7.1 fusion.88
  1750.6 8.8 fusion.94
  1759.4 3.5 all-to-all-start.1
  1762.9 44.2 all-gather.1
  1810.3 3.5 all-to-all-start.2
  1814.6 13.0 all-to-all-done.2
  1827.5 9.1 fusion.81
  1838.4 5.9 fusion.97
  1844.3 3.6 all-to-all-start.3
  1848.4 11.1 all-to-all-done.3
  1861.2 2.2 convert_add_fusion.1
  1864.8 7.0 fusion.90
  1871.7 20.6 copy.100
  1892.3 6.7 copy.120
  1899.1 8.3 fusion.91
  1907.6 5.2 all-gather.2
  1915.3 5.8 all_gather.68
  1925.0 2602.1 %while.53 = (s32[]{:T(128)}, f32[256,12,64]{0,2,1:T(8,128)}, f32[32,12]{0,1:T(8,128)}, bf16[1024,768]{0,1:T(8,128)(2,1)}, s32[256]{0:T(256)S(1)}, /*index=5*/s32...) while((s32[]{:T(128)}, f32[256,12,64]{0,2,1:T(8,128)}, ...), condition=%wide.region_16.18_spmd.clone, body=%wide.region_15.17_spmd.clone.sunk | while | flops 825624064 | bytes 75947520 | solution.py:284
  1927.8 1278.2 %gather_fusion.1 = s32[131072]{0:T(1024)} fusion(s32[2047]{0:T(1024)S(1)} %get-tuple-element.1512, s32[131072]{0:T(1024)} %broadcast_clamp_fusion.7), kind=kCustom, calls=%fused_computation.2.clone.clone.1 | custom fusion | bytes 1572864 | tf_op jit(solution)/shard_map/while/body/eval_jaxpr/jit(_take)/gather | solution.py:52
  3213.4 2.5 fusion.251
  3216.0 4.6 fusion.253
  3220.7 3.8 fusion.255
  3228.8 1278.2 %gather_fusion.1 = s32[131072]{0:T(1024)} fusion(s32[2047]{0:T(1024)S(1)} %get-tuple-element.1512, s32[131072]{0:T(1024)} %broadcast_clamp_fusion.7), kind=kCustom, calls=%fused_computation.2.clone.clone.1 | custom fusion | bytes 1572864 | tf_op jit(solution)/shard_map/while/body/eval_jaxpr/jit(_take)/gather | solution.py:52
  4514.4 2.5 fusion.251
  4517.0 4.6 fusion.253
  4521.7 3.8 fusion.255
  4528.3 5.7 all_gather.70
  4533.9 3.0 fusion.133
  4537.1 1501.2 %while.54 = (s32[]{:T(128)}, f32[256,12,64]{0,2,1:T(8,128)}, f32[256,12,64]{0,2,1:T(8,128)}, bf16[1024,768]{1,0:T(8,128)(2,1)}, f32[1024]{0:T(1024)}, /*index=5*...) while((s32[]{:T(128)}, f32[256,12,64]{0,2,1:T(8,128)}, ...), condition=%wide.region_18.20_spmd.clone, body=%wide.region_17.19_spmd.clone.sunk | while | flops 924058880 | bytes 66654592 | solution.py:347
  4540.8 724.9 %gather_fusion.2 = s32[131072]{0:T(1024)S(1)} fusion(s32[2047]{0:T(1024)S(1)} %get-tuple-element.1566, s32[131072]{0:T(1024)S(1)} %broadcast_clamp_fusion.8), kind=kCustom, calls=%fused_computation.1.clone.clone.1 | custom fusion | bytes 1572864 | tf_op jit(solution)/shard_map/while/body/eval_jaxpr/jit(_take)/gather | solution.py:52
  5268.2 2.5 fusion.266
  5270.7 7.4 fusion.267
  5278.1 4.9 fusion.268
  5283.0 3.8 fusion.269
  5291.4 724.9 %gather_fusion.2 = s32[131072]{0:T(1024)S(1)} fusion(s32[2047]{0:T(1024)S(1)} %get-tuple-element.1566, s32[131072]{0:T(1024)S(1)} %broadcast_clamp_fusion.8), kind=kCustom, calls=%fused_computation.1.clone.clone.1 | custom fusion | bytes 1572864 | tf_op jit(solution)/shard_map/while/body/eval_jaxpr/jit(_take)/gather | solution.py:52
  6018.7 2.6 fusion.266
  6021.3 7.4 fusion.267
  6028.7 4.9 fusion.268
  6033.6 3.8 fusion.269
  6039.7 2.7 fusion.129
  6051.3 37.7 all-reduce.5
  6099.2 38.9 reduce-scatter.14.cloned.1.call-done
  6138.1 104.6 %reduce-scatter.12.cloned.1.call-done = f32[24,768]{1,0:T(8,128)} async-done(((f32[768,768]{1,0:T(8,128)}), f32[24,768]{1,0:T(8,128)}) %reduce-scatter.12.cloned.1.call-update) | async-done | bytes 73744 | tf_op jit(solution)/shard_map/reduce_scatter | solution.py:367
  (513 shorter events, 103.0 us)
Async XLA Ops:
  7.2 172.5 %copy-start.19 = (bf16[256,768]{1,0:T(8,128)(2,1)S(1)}, bf16[256,768]{1,0:T(8,128)(2,1)}, u32[]{:S(2)}) copy-start(bf16[256,768]{1,0:T(8,128)(2,1)} %param.23) | copy-start | bytes 1179652
  7.2 121.9 %copy-start.61 = (s32[256]{0:T(256)S(1)}, s32[256]{0:T(256)}, u32[]{:S(2)}) copy-start(s32[256]{0:T(256)} %param.24) | copy-start | bytes 3076
  7.2 127.2 %copy-start.85 = (s32[256,1]{0,1:T(1,128)S(1)}, s32[256,1]{0,1:T(1,128)}, u32[]{:S(2)}) copy-start(s32[256,1]{0,1:T(1,128)} %param.26) | copy-start | bytes 3076
  7.2 60.6 all-gather.20.cloned.1.call-start
  7.9 115.8 %all-gather.14.cloned.1.call-start = ((), (), s32[]{:S(2)}) async-start(), calls=%async_computation.10 | async-start | bytes 1216512 | tf_op jit(solution)/shard_map/all_gather | solution.py:98
  8.7 171.0 %all-gather.18.cloned.1.call-start = ((), (), s32[]{:S(2)}) async-start(), calls=%async_computation.12 | async-start | bytes 1216512 | tf_op jit(solution)/shard_map/all_gather | solution.py:97
  9.4 190.3 %all-gather.22.cloned.1.call-start = ((), (), s32[]{:S(2)}) async-start(), calls=%async_computation.14 | async-start | bytes 1966080 | tf_op jit(solution)/shard_map/all_gather | solution.py:149
  53.2 149.0 %copy-start.68 = (f32[768]{0:T(1024)}, f32[768]{0:T(1024)S(1)}, u32[]{:S(2)}) copy-start(f32[768]{0:T(1024)S(1)} %convert_element_type.178) | copy-start | bytes 9220
  54.4 74.7 %copy-start.107 = (f32[256]{0:T(256)}, f32[256]{0:T(256)S(1)}, u32[]{:S(2)}) copy-start(f32[256]{0:T(256)S(1)} %fusion.108) | copy-start | bytes 3076
  54.4 147.8 %copy-start.83 = (f32[256]{0:T(256)}, f32[256]{0:T(256)S(1)}, u32[]{:S(2)}) copy-start(f32[256]{0:T(256)S(1)} %fusion.125) | copy-start | bytes 3076
  70.5 153.4 %copy-start = (s32[2047]{0:T(1024)S(1)}, s32[2047]{0:T(1024)}, u32[]{:S(2)}) copy-start(s32[2047]{0:T(1024)} %param.25) | copy-start | bytes 24568
  70.6 150.8 %all-gather.16.cloned.1.call-start = ((), (), s32[]{:S(2)}) async-start(), calls=%async_computation.11 | async-start | bytes 1966080 | tf_op jit(solution)/shard_map/all_gather | solution.py:148
  126.4 1599.4 %all-gather.24.cloned.1.call-start = ((), (), s32[]{:S(2)}) async-start(), calls=%async_computation.15 | async-start | bytes 1216512 | tf_op jit(solution)/shard_map/all_gather | solution.py:100
  127.0 1616.4 %all-gather.26.cloned.1.call-start = ((), (), s32[]{:S(2)}) async-start(), calls=%async_computation.16 | async-start | bytes 5308416 | tf_op jit(solution)/shard_map/all_gather | solution.py:111
  127.7 1622.9 %all-gather.28.cloned.1.call-start = ((), (), s32[]{:S(2)}) async-start(), calls=%async_computation.17 | async-start | bytes 5308416 | tf_op jit(solution)/shard_map/all_gather | solution.py:112
  181.5 42.5 copy-start.39
  224.0 1501.9 %copy-start.20 = (bf16[256,768]{1,0:T(8,128)(2,1)S(1)}, bf16[256,768]{1,0:T(8,128)(2,1)}, u32[]{:S(2)}) copy-start(bf16[256,768]{1,0:T(8,128)(2,1)} %param.23) | copy-start | bytes 1179652
  224.0 1503.9 %copy-start.80 = (f32[768]{0:T(1024)S(1)}, f32[768]{0:T(1024)}, u32[]{:S(2)}) copy-start(f32[768]{0:T(1024)} %convert_element_type.185) | copy-start | bytes 9220
  225.4 725.0 %copy-start.58 = (s32[512]{0:T(512)S(1)}, s32[512]{0:T(512)}, u32[]{:S(2)}) copy-start(s32[512]{0:T(512)} %copy-done.57) | copy-start | bytes 6148 | tf_op jit(solution)/shard_map/while
  225.4 725.0 %copy-start.76 = (s32[256]{0:T(256)S(1)}, s32[256]{0:T(256)}, u32[]{:S(2)}) copy-start(s32[256]{0:T(256)} %copy-done.75) | copy-start | bytes 3076 | tf_op jit(solution)/shard_map/while
  225.4 725.2 %copy-start.1 = (bf16[1024,768]{0,1:T(8,128)(2,1)S(1)}, bf16[1024,768]{0,1:T(8,128)(2,1)}, u32[]{:S(2)}) copy-start(bf16[1024,768]{0,1:T(8,128)(2,1)} %get-tuple-element.1463) | copy-start | bytes 4718596 | tf_op jit(solution)/shard_map/while
  225.4 726.5 %copy-start.45 = (bf16[32,12]{0,1:T(8,128)(2,1)S(1)}, bf16[32,12]{0,1:T(8,128)(2,1)}, u32[]{:S(2)}) copy-start(bf16[32,12]{0,1:T(8,128)(2,1)} %get-tuple-element.1462) | copy-start | bytes 2308 | tf_op jit(solution)/shard_map/while
  975.4 725.0 %copy-start.58 = (s32[512]{0:T(512)S(1)}, s32[512]{0:T(512)}, u32[]{:S(2)}) copy-start(s32[512]{0:T(512)} %copy-done.57) | copy-start | bytes 6148 | tf_op jit(solution)/shard_map/while
  975.4 725.0 %copy-start.76 = (s32[256]{0:T(256)S(1)}, s32[256]{0:T(256)}, u32[]{:S(2)}) copy-start(s32[256]{0:T(256)} %copy-done.75) | copy-start | bytes 3076 | tf_op jit(solution)/shard_map/while
  975.4 725.2 %copy-start.1 = (bf16[1024,768]{0,1:T(8,128)(2,1)S(1)}, bf16[1024,768]{0,1:T(8,128)(2,1)}, u32[]{:S(2)}) copy-start(bf16[1024,768]{0,1:T(8,128)(2,1)} %get-tuple-element.1463) | copy-start | bytes 4718596 | tf_op jit(solution)/shard_map/while
  975.4 726.5 %copy-start.45 = (bf16[32,12]{0,1:T(8,128)(2,1)S(1)}, bf16[32,12]{0,1:T(8,128)(2,1)}, u32[]{:S(2)}) copy-start(bf16[32,12]{0,1:T(8,128)(2,1)} %get-tuple-element.1462) | copy-start | bytes 2308 | tf_op jit(solution)/shard_map/while
  1728.0 79.2 %copy-start.27 = (bf16[256,768]{1,0:T(8,128)(2,1)}, bf16[256,768]{1,0:T(8,128)(2,1)S(1)}, u32[]{:S(2)}) copy-start(bf16[256,768]{1,0:T(8,128)(2,1)S(1)} %multiply_convert_fusion.7) | copy-start | bytes 1179652
  1750.6 57.1 copy-start.33
  1750.6 57.1 copy-start.95
  1750.6 58.4 copy-start.86
  1759.4 48.2 all-to-all-start.1
  1807.3 29.3 copy-start.81
  1807.5 29.1 copy-start.89
  1807.6 52.4 copy-start.78
  1807.6 29.0 copy-start.92
  1808.9 27.7 copy-start.97
  1809.0 27.7 copy-start.106
  1810.3 17.2 all-to-all-start.2
  1813.8 2723.2 %all-gather.30.cloned.1.call-start = ((), (), s32[]{:S(2)}) async-start(), calls=%async_computation.18 | async-start | bytes 1966080 | tf_op jit(solution)/shard_map/all_gather | solution.py:308
  1838.4 22.8 copy-start.103
  1844.3 15.3 all-to-all-start.3
  1847.9 2689.2 %all-gather.32.cloned.1.call-start = ((), (), s32[]{:S(2)}) async-start(), calls=%async_computation.19 | async-start | bytes 1966080 | tf_op jit(solution)/shard_map/all_gather | solution.py:309
  1863.4 59.4 copy-start.25
  1864.7 4227.8 %reduce-scatter.20.cloned.1.call-start = ((), (), s32[]{:S(2)}) async-start(), calls=%async_computation.25 | async-start | bytes 5308416
  1899.1 4197.9 %reduce-scatter.18.cloned.1.call-start = ((), (), s32[]{:S(2)}) async-start(), calls=%async_computation.24 | async-start | bytes 5308416 | tf_op jit(solution)/shard_map/reduce_scatter | solution.py:378
  1907.5 4191.7 %reduce-scatter.16.cloned.1.call-start = ((), (), s32[]{:S(2)}) async-start(), calls=%async_computation.23 | async-start | bytes 2433024 | tf_op jit(solution)/shard_map/reduce_scatter | solution.py:369
  1924.8 4174.4 %reduce-scatter.10.cloned.1.call-start = ((), (), s32[]{:S(2)}) async-start(), calls=%async_computation.20 | async-start | bytes 2433024 | tf_op jit(solution)/shard_map/reduce_scatter | solution.py:366
  1925.0 1281.0 %copy-start.64 = (s32[256]{0:T(256)}, s32[256]{0:T(256)S(1)}, u32[]{:S(2)}) copy-start(s32[256]{0:T(256)S(1)} %get-tuple-element.1509) | copy-start | bytes 3076 | tf_op jit(solution)/shard_map/while
  1927.8 1280.2 %copy-start.60 = (s32[512]{0:T(512)S(1)}, s32[512]{0:T(512)}, u32[]{:S(2)}) copy-start(s32[512]{0:T(512)} %copy-done.59) | copy-start | bytes 6148 | tf_op jit(solution)/shard_map/while
  1927.8 1284.3 %copy-start.2 = (bf16[1024,768]{0,1:T(8,128)(2,1)S(1)}, bf16[1024,768]{0,1:T(8,128)(2,1)}, u32[]{:S(2)}) copy-start(bf16[1024,768]{0,1:T(8,128)(2,1)} %get-tuple-element.1515) | copy-start | bytes 4718596 | tf_op jit(solution)/shard_map/while
  1927.8 1284.3 %copy-start.3 = (bf16[1024,768]{0,1:T(8,128)(2,1)S(1)}, bf16[1024,768]{0,1:T(8,128)(2,1)}, u32[]{:S(2)}) copy-start(bf16[1024,768]{0,1:T(8,128)(2,1)} %get-tuple-element.1508) | copy-start | bytes 4718596 | tf_op jit(solution)/shard_map/while
  3226.1 1281.0 %copy-start.64 = (s32[256]{0:T(256)}, s32[256]{0:T(256)S(1)}, u32[]{:S(2)}) copy-start(s32[256]{0:T(256)S(1)} %get-tuple-element.1509) | copy-start | bytes 3076 | tf_op jit(solution)/shard_map/while
  3228.8 1280.2 %copy-start.60 = (s32[512]{0:T(512)S(1)}, s32[512]{0:T(512)}, u32[]{:S(2)}) copy-start(s32[512]{0:T(512)} %copy-done.59) | copy-start | bytes 6148 | tf_op jit(solution)/shard_map/while
  3228.8 1284.3 %copy-start.2 = (bf16[1024,768]{0,1:T(8,128)(2,1)S(1)}, bf16[1024,768]{0,1:T(8,128)(2,1)}, u32[]{:S(2)}) copy-start(bf16[1024,768]{0,1:T(8,128)(2,1)} %get-tuple-element.1515) | copy-start | bytes 4718596 | tf_op jit(solution)/shard_map/while
  3228.8 1284.3 %copy-start.3 = (bf16[1024,768]{0,1:T(8,128)(2,1)S(1)}, bf16[1024,768]{0,1:T(8,128)(2,1)}, u32[]{:S(2)}) copy-start(bf16[1024,768]{0,1:T(8,128)(2,1)} %get-tuple-element.1508) | copy-start | bytes 4718596 | tf_op jit(solution)/shard_map/while
  4537.0 1601.1 %reduce-scatter.14.cloned.1.call-start = ((), (), s32[]{:S(2)}) async-start(), calls=%async_computation.22 | async-start | bytes 2433024 | tf_op jit(solution)/shard_map/reduce_scatter | solution.py:368
  4537.1 1502.6 %copy-start.21 = (bf16[256,768]{1,0:T(8,128)(2,1)S(1)}, bf16[256,768]{1,0:T(8,128)(2,1)}, u32[]{:S(2)}) copy-start(bf16[256,768]{1,0:T(8,128)(2,1)} %param.23) | copy-start | bytes 1179652
  4537.1 1502.6 %copy-start.69 = (f32[768]{0:T(1024)S(1)}, f32[768]{0:T(1024)}, u32[]{:S(2)}) copy-start(f32[768]{0:T(1024)} %copy-done.68) | copy-start | bytes 9220
  4540.8 725.1 %copy-start.56 = (s32[512]{0:T(512)S(1)}, s32[512]{0:T(512)}, u32[]{:S(2)}) copy-start(s32[512]{0:T(512)} %copy-done.55) | copy-start | bytes 6148 | tf_op jit(solution)/shard_map/while
  4540.8 725.1 %copy-start.74 = (s32[256]{0:T(256)S(1)}, s32[256]{0:T(256)}, u32[]{:S(2)}) copy-start(s32[256]{0:T(256)} %copy-done.73) | copy-start | bytes 3076 | tf_op jit(solution)/shard_map/while
  5291.3 725.1 %copy-start.56 = (s32[512]{0:T(512)S(1)}, s32[512]{0:T(512)}, u32[]{:S(2)}) copy-start(s32[512]{0:T(512)} %copy-done.55) | copy-start | bytes 6148 | tf_op jit(solution)/shard_map/while
  5291.3 725.1 %copy-start.74 = (s32[256]{0:T(256)S(1)}, s32[256]{0:T(256)}, u32[]{:S(2)}) copy-start(s32[256]{0:T(256)} %copy-done.73) | copy-start | bytes 3076 | tf_op jit(solution)/shard_map/while
  6042.4 200.3 %reduce-scatter.12.cloned.1.call-start = ((), (), s32[]{:S(2)}) async-start(), calls=%async_computation.21 | async-start | bytes 2433024 | tf_op jit(solution)/shard_map/reduce_scatter | solution.py:367
  6044.8 46.8 copy-start.26
  (115 other events, 665.4 us)
Sparse Core Ops, SparseCore 0:
  10.9 56.8 all-gather.19
  70.7 52.9 all-gather.13
  126.6 52.9 all-gather.17
  181.1 18.5 all-gather.21
  201.7 19.6 all-gather.15
  224.1 54.0 all-gather.23
  280.3 79.9 all-gather.25
  362.4 78.0 all-gather.27
  1816.2 19.1 all-gather.29
  1864.9 15.7 all-gather.31
  1899.2 91.5 reduce-scatter.19
  1994.2 95.1 reduce-scatter.17
  2095.3 98.6 reduce-scatter.15
  4537.1 95.6 reduce-scatter.9
  6042.5 95.5 reduce-scatter.13
  6144.7 98.0 reduce-scatter.11
where the time goes:
time: 6250 us
  local copies, waits for them, and re-layouts  5550 us (89%)
  waiting for transfers between devices  319 us (5%)
  matrix products  163 us (3%)
  blocking collectives  160 us (3%)
    gather x12, local copies, waits for them, and re-layouts, bucket_onehot(): ids = jnp.take(buckets, index, axis=0)  5460 us
  transfers between devices with their start and end apart: 19, of which 9 were waited for; matrix products, arithmetic and copies ran while one was open for 92% of the time, Pallas kernels for 0%

commit v1 on v0

v1 whole, which is shorter than its diff:
```python
import functools

import jax
import jax.numpy as jnp
from jax import lax
from jax.experimental import pallas as pl
from jax.experimental.pallas import tpu as pltpu
from jax.sharding import PartitionSpec as P

HEADS = 12
HEAD = 64
BUCKETS = 32
LANES = 128
SUBLANES = 8

EPSILON = 1e-06
MASKED = -1000000000.0
HIGHEST = lax.Precision.HIGHEST
BF16 = jnp.bfloat16
F32 = jnp.float32


def inverse_rms(values):
    return lax.rsqrt(jnp.mean(values * values, axis=-1, keepdims=True) + EPSILON)


def norm_gradient(grad, gain, unit, scale):
    inner = grad * gain
    return scale * (inner - unit * jnp.mean(inner * unit, axis=-1, keepdims=True))


def gelu_tanh(values):
    return jax.nn.gelu(values, approximate=True)


def product(left, right):
    return jnp.dot(left, right, preferred_element_type=F32)


def contract(left, left_dim, right, right_dim, precision=None):
    return lax.dot_general(
        left,
        right,
        (((left_dim,), (right_dim,)), ((), ())),
        precision=precision,
        preferred_element_type=F32,
    )


def attend_kernel(off_ref, seg_query_ref, seg_key_ref, q_ref, k_ref, v_ref, o_ref, p_ref, skew_ref):
    turn = pl.program_id(1)
    rows = q_ref.shape[1]
    group = k_ref.shape[1]
    width = skew_ref.shape[1]

    @pl.when(turn == 0)
    def _():
        wide = jnp.broadcast_to(off_ref[0], (LANES, width))
        skew_ref[...] = pltpu.roll(wide, width - (LANES - 1), 1, stride=1, stride_axis=0)

    scores = contract(q_ref[0], 1, k_ref[0], 1)
    for part in range(rows // LANES):
        here = slice(part * LANES, (part + 1) * LANES)
        start = group - LANES - turn * rows - part * LANES
        bias = skew_ref[:, pl.ds(pl.multiple_of(start, LANES), group)]
        keep = seg_query_ref[here, :] == seg_key_ref[...]
        biased = jnp.where(keep, scores[here] + bias, MASKED)
        top = jnp.max(biased, axis=1, keepdims=True)
        weights = jnp.exp(biased - top)
        total = jnp.sum(weights, axis=1, keepdims=True)
        probs = (weights * (1.0 / total)).astype(BF16)
        p_ref[0, here, :] = probs
        o_ref[0, here, :] = product(probs, v_ref[0]).astype(BF16)


def attend_back_kernel(
    p_ref, do_ref, q_ref, k_ref, v_ref, dq_ref, dk_ref, dv_ref, doff_ref, dk_acc, dv_acc, diag
):
    turn = pl.program_id(1)
    rows = q_ref.shape[1]
    group = k_ref.shape[1]
    width = diag.shape[1]

    @pl.when(turn == 0)
    def _():
        dk_acc[...] = jnp.zeros_like(dk_acc)
        dv_acc[...] = jnp.zeros_like(dv_acc)
        diag[...] = jnp.zeros_like(diag)

    probs = p_ref[0]
    grad = do_ref[0]
    grad_probs = contract(grad, 1, v_ref[0], 1)
    wide = probs.astype(F32)
    correction = jnp.sum(wide * grad_probs, axis=1, keepdims=True)
    grad_scores = (wide * (grad_probs - correction)).astype(BF16)
    dq_ref[0] = product(grad_scores, k_ref[0]).T.astype(BF16)
    dk_acc[...] += contract(q_ref[0], 0, grad_scores, 0)
    dv_acc[...] += contract(grad, 0, probs, 0)
    for part in range(rows // LANES):
        start = group - LANES - turn * rows - part * LANES
        there = pl.ds(pl.multiple_of(start, LANES), group)
        diag[:, there] += grad_scores[part * LANES : (part + 1) * LANES, :].astype(F32)

    @pl.when(turn == pl.num_programs(1) - 1)
    def _():
        dk_ref[0] = dk_acc[...].astype(BF16)
        dv_ref[0] = dv_acc[...].astype(BF16)
        lined = jnp.zeros((SUBLANES, width), F32)
        for first in range(0, LANES, SUBLANES):
            lined += pltpu.roll(diag[first : first + SUBLANES, :], LANES - 1 - first, 1)
        row = lax.broadcasted_iota(jnp.int32, lined.shape, 0)
        for bit in (1, 2, 4):
            lined = jnp.where((row & bit) != 0, pltpu.roll(lined, width - bit, 1), lined)
        doff_ref[0] = jnp.sum(lined, axis=0, keepdims=True)


VMEM_LIMIT = 50 * 1024 * 1024


def attend(offsets, segment, queries, keys, values):
    heads, group, size = queries.shape
    width = offsets.shape[-1]
    rows = min(256, group)
    one = pl.BlockSpec((1, group, size), lambda h, b: (h, 0, 0))
    block = pl.BlockSpec((1, rows, size), lambda h, b: (h, b, 0))
    return pl.pallas_call(
        attend_kernel,
        grid=(heads, group // rows),
        in_specs=[
            pl.BlockSpec((1, 1, width), lambda h, b: (h, 0, 0)),
            pl.BlockSpec((rows, 1), lambda h, b: (b, 0)),
            pl.BlockSpec((1, group), lambda h, b: (0, 0)),
            block,
            one,
            one,
        ],
        out_specs=[block, pl.BlockSpec((1, rows, group), lambda h, b: (h, b, 0))],
        out_shape=[
            jax.ShapeDtypeStruct((heads, group, size), BF16),
            jax.ShapeDtypeStruct((heads, group, group), BF16),
        ],
        scratch_shapes=[pltpu.VMEM((LANES, width), F32)],
        compiler_params=pltpu.CompilerParams(vmem_limit_bytes=VMEM_LIMIT),
        cost_estimate=pl.CostEstimate(
            flops=16 * heads * group * group * size,
            bytes_accessed=2 * heads * group * (group + 4 * size),
            transcendentals=heads * group * group,
        ),
        name="attend",
    )(offsets.reshape(heads, 1, width), segment[:, None], segment[None, :], queries, keys, values)


def attend_back(probs, grads, queries, keys, values, width):
    heads, group, size = queries.shape
    rows = min(256, group)
    one = pl.BlockSpec((1, group, size), lambda h, b: (h, 0, 0))
    block = pl.BlockSpec((1, rows, size), lambda h, b: (h, b, 0))
    across = pl.BlockSpec((1, size, group), lambda h, b: (h, 0, 0))
    turned = jax.ShapeDtypeStruct((heads, size, group), BF16)
    return pl.pallas_call(
        attend_back_kernel,
        grid=(heads, group // rows),
        in_specs=[
            pl.BlockSpec((1, rows, group), lambda h, b: (h, b, 0)),
            block,
            block,
            one,
            one,
        ],
        out_specs=[
            pl.BlockSpec((1, size, rows), lambda h, b: (h, 0, b)),
            across,
            across,
            pl.BlockSpec((1, 1, width), lambda h, b: (h, 0, 0)),
        ],
        out_shape=[
            turned,
            turned,
            turned,
            jax.ShapeDtypeStruct((heads, 1, width), F32),
        ],
        scratch_shapes=[
            pltpu.VMEM((size, group), F32),
            pltpu.VMEM((size, group), F32),
            pltpu.VMEM((LANES, width), F32),
        ],
        compiler_params=pltpu.CompilerParams(vmem_limit_bytes=VMEM_LIMIT),
        cost_estimate=pl.CostEstimate(
            flops=32 * heads * group * group * size,
            bytes_accessed=2 * heads * group * (group + 8 * size),
            transcendentals=0,
        ),
        name="attend_back",
    )(probs, grads, queries, keys, values)


def exchange(blocks):
    return lax.all_to_all(blocks, "fsdp", split_axis=0, concat_axis=0, tiled=True)


def total_everywhere(part):
    for axis in ("fsdp", "dp"):
        size = lax.axis_size(axis)
        step = 1
        while step < size:
            part = part + lax.ppermute(part, axis, [(i, i ^ step) for i in range(size)])
            step *= 2
    return part


def pad_lanes(array):
    short = -array.shape[-1] % LANES
    return jnp.pad(array, [(0, 0)] * (array.ndim - 1) + [(0, short)])


def body(
    tokens,
    segment,
    buckets,
    routes,
    w_query,
    w_key,
    w_value,
    w_output,
    w_router,
    norm_attn,
    norm_ffn,
    bias_table,
    expert_in,
    expert_out,
    out_grad,
):
    tok_rows, model = tokens.shape
    shard_rows = w_query.shape[0]
    peers = lax.axis_size("fsdp")
    group = tok_rows * peers
    capacity = 2 * tok_rows // peers
    heads = -(-HEADS // peers)
    own_cols = heads * HEAD
    all_cols = peers * own_cols
    me = lax.axis_index("fsdp")

    def by_peer(matrix):
        padded = jnp.pad(matrix, ((0, 0), (0, all_cols - HEADS * HEAD)))
        return jnp.transpose(padded.reshape(matrix.shape[0], peers, own_cols), (1, 0, 2))

    rest = jnp.concatenate([w_output, w_router, norm_attn[:, None], norm_ffn[:, None]], axis=1)
    packed = pad_lanes(
        jnp.concatenate(
            [
                by_peer(w_query),
                by_peer(w_key),
                by_peer(w_value),
                jnp.broadcast_to(rest[None], (peers,) + rest.shape),
            ],
            axis=2,
        )
    )
    dense = exchange(packed).reshape(peers * shard_rows, packed.shape[-1])
    dense = lax.all_gather(dense, "dp", axis=0, tiled=True)
    qkv_cols = 3 * own_cols
    weight_qkv = dense[:, :qkv_cols]
    weight_output = dense[:, qkv_cols : qkv_cols + model]
    weight_router = dense[:, qkv_cols + model : qkv_cols + model + peers]
    gains = dense[:, qkv_cols + model + peers : qkv_cols + model + peers + 2].astype(F32).T
    gain_attn, gain_ffn = gains[0:1], gains[1:2]

    tokens_all = lax.all_gather(tokens, "fsdp", axis=0, tiled=True)
    segment_all = lax.all_gather(segment, "fsdp", axis=0, tiled=True)

    ff_rows = expert_out.shape[1]
    expert_pack = jnp.concatenate([expert_in[0].T, expert_out[0]], axis=1)
    expert_all = lax.all_gather(expert_pack, "dp", axis=0, tiled=True)
    weight_in = expert_all[:, :model]
    weight_out = expert_all[:, model:]

    route = routes[:, 0]
    picked = (route[:, None] == jnp.arange(peers, dtype=jnp.int32)[None, :]).astype(jnp.int32)
    picked_float = picked.astype(F32)
    rank = jnp.sum((jnp.cumsum(picked, axis=0) - 1) * picked, axis=1)
    slot = route * capacity + rank
    slots = peers * capacity
    placing = (jnp.arange(slots, dtype=jnp.int32)[:, None] == slot[None, :]).astype(BF16)

    def dispatch(rows):
        placed = product(placing, rows).astype(BF16).reshape(peers, capacity, rows.shape[-1])
        return exchange(placed).reshape(slots, rows.shape[-1])

    def give_back(rows):
        returned = exchange(rows.reshape(peers, capacity, rows.shape[-1]))
        return contract(placing, 0, returned.reshape(slots, rows.shape[-1]), 0)

    grad_arrived = dispatch(out_grad)

    bucket_hot = (
        jnp.pad(buckets, (0, 1), constant_values=-1)[:, None]
        == jnp.arange(BUCKETS, dtype=jnp.int32)[None, :]
    )
    table_pad = jnp.pad(bias_table, ((0, 0), (0, peers * heads - HEADS)))
    own_table = lax.dynamic_slice_in_dim(table_pad, me * heads, heads, 1)
    offsets = contract(own_table, 0, bucket_hot.astype(BF16), 1)

    wide_all = tokens_all.astype(F32)
    unit_all = wide_all * inverse_rms(wide_all)
    hidden = (unit_all * gain_attn).astype(BF16)
    qkv = product(hidden, weight_qkv).astype(BF16)
    qkv = jnp.transpose(qkv.reshape(group, 3, heads, HEAD), (1, 2, 0, 3))
    queries, keys, values = qkv[0], qkv[1], qkv[2]
    attended, probs = attend(offsets, segment_all, queries, keys, values)
    blocks = jnp.transpose(attended, (1, 0, 2)).reshape(peers, tok_rows, own_cols)
    attn_out = jnp.transpose(exchange(blocks), (1, 0, 2)).reshape(tok_rows, all_cols)
    attn_out = attn_out[:, : HEADS * HEAD]

    inputs = tokens.astype(F32)
    residual = inputs + product(attn_out, weight_output)
    scale_ffn = inverse_rms(residual)
    unit_ffn = residual * scale_ffn
    hidden2 = (unit_ffn * gain_ffn).astype(BF16)
    logits = product(hidden2, weight_router)
    chances = jax.nn.softmax(logits, axis=-1)
    gate = jnp.sum(chances * picked_float, axis=-1, keepdims=True)

    gate_high = gate.astype(BF16)
    gate_low = (gate - gate_high.astype(F32)).astype(BF16)
    arrived = dispatch(pad_lanes(jnp.concatenate([hidden2, gate_high, gate_low], axis=1)))
    gate_slots = jnp.sum(arrived[:, model : model + 2].astype(F32), axis=1, keepdims=True)
    arrived = arrived[:, :model]
    d_arrived = (gate_slots * grad_arrived.astype(F32)).astype(BF16)
    pre = contract(arrived, 1, weight_in, 1)
    activated, gelu_back = jax.vjp(gelu_tanh, pre)
    activated = activated.astype(BF16)
    result = product(activated, weight_out).astype(BF16)
    token_result = give_back(result)
    d_activated = contract(d_arrived, 1, weight_out, 1)
    d_pre = gelu_back(d_activated)[0].astype(BF16)
    d_rows = product(d_pre, weight_in).astype(BF16)
    d_from_expert = give_back(d_rows)
    d_weight_out = contract(activated, 0, d_arrived, 0).astype(BF16)
    d_weight_in = contract(d_pre, 0, arrived, 0).astype(BF16)
    d_expert_out = lax.psum_scatter(d_weight_out, "dp", scatter_dimension=0, tiled=True)
    d_expert_in = lax.psum_scatter(d_weight_in, "dp", scatter_dimension=0, tiled=True)

    mixed = residual + gate * token_result
    grad_out = out_grad.astype(F32)
    d_gate = jnp.sum(grad_out * token_result, axis=-1, keepdims=True)
    d_logits = (gate * (picked_float - chances) * d_gate).astype(BF16)
    d_hidden2 = d_from_expert + contract(d_logits, 1, weight_router, 1)
    d_router = contract(hidden2, 0, d_logits, 0)
    d_gain_ffn = jnp.sum(d_hidden2 * unit_ffn, axis=0)
    d_residual = grad_out + norm_gradient(d_hidden2, gain_ffn, unit_ffn, scale_ffn)
    d_branch = d_residual.astype(BF16)
    d_weight_output = contract(attn_out, 0, d_branch, 0)
    d_attended = contract(d_branch, 1, weight_output, 1).astype(BF16)

    d_blocks = exchange(by_peer(d_attended)).reshape(group, heads, HEAD)
    d_heads = jnp.transpose(d_blocks, (1, 0, 2))
    d_queries, d_keys, d_values, d_offsets = attend_back(
        probs, d_heads, queries, keys, values, offsets.shape[-1]
    )
    d_table = contract(
        bucket_hot.astype(F32), 0, d_offsets.reshape(heads, offsets.shape[-1]), 1, HIGHEST
    )
    d_table = lax.dynamic_update_slice_in_dim(
        jnp.zeros((BUCKETS, peers * heads), F32), d_table, me * heads, 1
    )
    table_total = total_everywhere(d_table)[:, :HEADS]
    d_qkv = jnp.concatenate([d_queries, d_keys, d_values], axis=0).reshape(qkv_cols, group)
    d_hidden_part = contract(d_qkv, 0, weight_qkv, 1)
    d_gain_attn = jnp.sum(d_hidden_part * unit_all, axis=0)
    d_weight_qkv = contract(hidden, 0, d_qkv, 1)
    d_hidden = exchange(d_hidden_part.astype(BF16).reshape(peers, tok_rows, model))
    d_hidden = jnp.sum(d_hidden.astype(F32), axis=0)
    scale_attn = inverse_rms(inputs)
    d_inputs = d_residual + norm_gradient(d_hidden, gain_attn, inputs * scale_attn, scale_attn)

    def reduce_rows(matrix):
        part = lax.psum_scatter(pad_lanes(matrix.astype(BF16)), "dp", scatter_dimension=0, tiled=True)
        return exchange(part.reshape(peers, shard_rows, part.shape[-1])).astype(F32)

    rest_rows = reduce_rows(
        jnp.concatenate([d_weight_output, d_router, d_gain_ffn[:, None]], axis=1)
    )
    rest_rows = jnp.sum(rest_rows, axis=0)
    qkv_rows = reduce_rows(jnp.concatenate([d_weight_qkv, d_gain_attn[:, None]], axis=1))
    gain_attn_rows = jnp.sum(qkv_rows[:, :, qkv_cols], axis=0)

    def from_peers(turn):
        cols = qkv_rows[:, :, turn * own_cols : (turn + 1) * own_cols]
        return jnp.transpose(cols, (1, 0, 2)).reshape(shard_rows, all_cols)[:, : HEADS * HEAD]

    return (
        mixed.astype(BF16),
        d_inputs.astype(BF16),
        from_peers(0),
        from_peers(1),
        from_peers(2),
        rest_rows[:, :model],
        rest_rows[:, model : model + peers],
        gain_attn_rows,
        rest_rows[:, model + peers],
        table_total,
        d_expert_in.astype(F32).T[None],
        d_expert_out.astype(F32)[None],
    )


def solution(mesh):
    rows = P(("dp", "fsdp"), None)
    flat = P(("dp", "fsdp"))
    return jax.shard_map(
        body,
        mesh=mesh,
        in_specs=(
            rows,
            flat,
            P(),
            rows,
            rows,
            rows,
            rows,
            rows,
            rows,
            flat,
            flat,
            P(),
            P("fsdp", None, "dp"),
            P("fsdp", "dp", None),
            rows,
        ),
        out_specs=(
            rows,
            rows,
            rows,
            rows,
            rows,
            rows,
            rows,
            flat,
            flat,
            P(),
            P("fsdp", None, "dp"),
            P("fsdp", "dp", None),
        ),
        check_vma=False,
    )
```

time: 6250 us -> 655 us (0.10)
  local copies, waits for them, and re-layouts: 5550 us -> 34 us
  blocking collectives: 160 us -> 27.9 us
  waiting for transfers between devices: 319 us -> 419 us
  matrix products: 163 us -> 64.4 us
    gather x12 -> x0, local copies, waits for them, and re-layouts: 5460 us -> none  [bucket_onehot(): ids = jnp.take(buckets, index, axis=0)]
    reduce_scatter x5 -> x4, waiting for transfers between devices: 144 us -> 243 us  [the longest x1 96.7 us: body(): lax.psum_scatter(d_weight_out, 'dp', scatter_dimension=0, tiled=True)]
    dot_general x49 -> x21, matrix products: 163 us -> 64.4 us  [the longest x14 43 us: contract(): lax.dot_general(left, right, (((left_dim,), (right_dim,)), ((), ())), pre...]
    unnamed x2 -> x0, blocking collectives: 79.8 us -> none
    all_gather x10 -> x3, waiting for transfers between devices: 146 us -> 107 us  [the longest x1 59.1 us: body(): expert_all = lax.all_gather(expert_pack, 'dp', axis=0, tiled=True)]
  transfers between devices with their start and end apart: 19 -> 20, of which waited for: 9 -> 16; matrix products, arithmetic and copies ran while one was open for 92% -> 14% of each run, Pallas kernels for 0% -> 2%
where the time goes in v1:
time: 655 us; the launch traced here: 647 us
  waiting for transfers between devices  419 us (64%)
  matrix products  64.4 us (10%)
  starting transfers between devices  35.2 us (5%)
  local copies, waits for them, and re-layouts  34 us (5%)
  blocking collectives  27.9 us (4%)
  Pallas kernels  27.4 us (4%)
  other arithmetic  23.5 us (4%)
  between operations  15.3 us (2%)
    reduce_scatter x1, waiting for transfers between devices, body(): lax.psum_scatter(d_weight_out, 'dp', scatter_dimension=0, tiled=True)  96.7 us
    reduce_scatter x1, waiting for transfers between devices, body(): lax.psum_scatter(d_weight_in, 'dp', scatter_dimension=0, tiled=True)  87.8 us
    all_gather x1, waiting for transfers between devices, body(): expert_all = lax.all_gather(expert_pack, 'dp', axis=0, tiled=True)  59.1 us
    reduce_scatter x2, waiting for transfers between devices, reduce_rows(): lax.psum_scatter(pad_lanes(matrix.astype(BF16)), 'dp', scatter_dimension=...  58.6 us
    all_gather x1, waiting for transfers between devices, body(): dense = lax.all_gather(dense, 'dp', axis=0, tiled=True)  48 us
    dot_general x14, matrix products, contract(): lax.dot_general(left, right, (((left_dim,), (right_dim,)), ((), ())), pre...  43 us
    all_to_all x8, waiting for transfers between devices, exchange(): lax.all_to_all(blocks, 'fsdp', split_axis=0, concat_axis=0, tiled=True)  41.1 us
    all_to_all x8, starting transfers between devices, exchange(): lax.all_to_all(blocks, 'fsdp', split_axis=0, concat_axis=0, tiled=True)  30.2 us
  transfers between devices with their start and end apart: 20, of which 16 were waited for; matrix products, arithmetic and copies ran while one was open for 14% of the time, Pallas kernels for 2%

profile of v1, /device:TPU:0, one launch (start us, length us, event | category | flops | bytes accessed | tf_op | source)
XLA Modules:
  0.0 646.7 jit_solution(13711392704594180409)
XLA Ops:
  14.1 12.8 %all_to_all.50 = bf16[4,24,1408]{2,1,0:T(8,128)(2,1)} all-to-all(bf16[4,24,1408]{2,1,0:T(8,128)(2,1)S(1)} %pad.21), channel_id=1, replica_groups=mesh['dp'=8,'fsdp'=4] {'fsdp'}, dimensions={0} | all-to-all | bytes 540672 | tf_op jit(solution)/shard_map/all_to_all | solution.py:198
  28.4 1.2 reduce-window.6
  30.5 5.1 all-gather
  37.2 1.8 fusion.19
  39.0 48.0 %all-gather.7.cloned.1.call-done = bf16[768,1408]{1,0:T(8,128)(2,1)} async-done(((bf16[96,1408]{1,0:T(8,128)(2,1)}), bf16[768,1408]{1,0:T(8,128)(2,1)}) %all-gather.7.cloned.1.call-update) | async-done | bytes 2162704 | tf_op jit(solution)/shard_map/all_gather | solution.py:260
  88.5 3.0 convolution_convert_fusion.3
  91.5 2.4 copy.167
  93.9 2.0 slice_bitcast_fusion
  95.9 12.8 %attend.1 = (bf16[3,1024,64]{2,1,0:T(8,128)(2,1)S(1)}, bf16[3,1024,1024]{2,1,0:T(8,128)(2,1)}) custom-call(f32[3,1,2048]{2,1,0:T(1,128)S(1)} %reshape.191.off_ref, s32[1024,1]{1,0:T(8,128)S(1)} %copy-done.3, s32[1,1024]{1,0:T(1,128)S(1)} %bitcast.101, bf16[3,1024,64]{2,1,0:T(8,128)(2,1)S(1)} %get-tuple-element.116.q_ref, ...), custom_call_target="tpu_custom_call" | custom-call | flops 3221225472 | bytes 7864320 | tf_op jit(solution)/shard_map/attend/pallas_call | solution.py:126
  110.0 3.5 all-to-all-start.1
  114.1 6.8 %all-to-all-done.1 = bf16[4,256,192]{1,2,0:T(8,128)(2,1)S(1)} async-done(((bf16[4,256,192]{1,2,0:T(8,128)(2,1)}), bf16[4,256,192]{1,2,0:T(8,128)(2,1)S(1)}, u32[]{:S(2)}, u32[]{:S(2)}) %all-to-all-start.1) | async-done | bytes 393248 | tf_op jit(solution)/shard_map/all_to_all | solution.py:198
  120.9 2.3 multiply_reduce_fusion.2
  123.9 1.4 fusion.86
  127.2 1.4 copy.173
  129.2 1.4 copy.174
  130.6 2.3 convolution_convert_fusion.4
  132.9 4.2 all-to-all-start.2
  137.2 2.0 convolution_convert_fusion.6
  139.1 11.1 %all-to-all-done.2 = bf16[4,128,896]{2,1,0:T(8,128)(2,1)} async-done(((bf16[4,128,896]{2,1,0:T(8,128)(2,1)}), bf16[4,128,896]{2,1,0:T(8,128)(2,1)}, u32[]{:S(2)}, u32[]{:S(2)}) %all-to-all-start.2) | async-done | bytes 917536 | tf_op jit(solution)/shard_map/all_to_all | solution.py:198
  150.3 3.7 all-to-all-start.4
  153.9 1.6 convert_reduce_fusion.2
  155.5 10.0 %all-to-all-done.4 = bf16[4,128,768]{2,1,0:T(8,128)(2,1)S(1)} async-done(((bf16[4,128,768]{2,1,0:T(8,128)(2,1)}), bf16[4,128,768]{2,1,0:T(8,128)(2,1)S(1)}, u32[]{:S(2)}, u32[]{:S(2)}) %all-to-all-start.4) | async-done | bytes 786464 | tf_op jit(solution)/shard_map/all_to_all | solution.py:198
  165.5 1.8 fusion.22
  167.3 59.1 %all-gather.9.cloned.1.call-done = bf16[3072,1536]{1,0:T(8,128)(2,1)} async-done(((bf16[384,1536]{1,0:T(8,128)(2,1)}), bf16[3072,1536]{1,0:T(8,128)(2,1)}) %all-gather.9.cloned.1.call-update) | async-done | bytes 9437200 | tf_op jit(solution)/shard_map/all_gather | solution.py:273
  226.4 4.9 fusion.13
  231.7 4.6 fusion.26
  236.3 3.5 all-to-all-start.3
  239.8 8.6 %fusion.6 = bf16[512,3072]{1,0:T(8,128)(2,1)S(1)} fusion(f32[512,3072]{1,0:T(8,128)} %copy-done.34, bf16[512,768]{1,0:T(8,128)(2,1)} %fusion.22, bf16[3072,1536]{1,0:T(8,128)(2,1)} %all-gather.9.cloned.1.call-done), kind=kOutput, calls=%fused_computation.8 | convolution fusion | flops 2447376384 | bytes 14942208 | tf_op jit(solution)/shard_map/dot_general | solution.py:41
  248.5 1.6 copy-done.35
  250.1 5.8 fusion.23
  256.0 4.2 all-to-all-start.5
  260.2 2.0 fusion.46
  262.8 1.3 fusion.71
  264.1 7.8 %all-to-all-done.5 = bf16[4,128,768]{2,1,0:T(8,128)(2,1)} async-done(((bf16[4,128,768]{2,1,0:T(8,128)(2,1)}), bf16[4,128,768]{2,1,0:T(8,128)(2,1)}, u32[]{:S(2)}, u32[]{:S(2)}) %all-to-all-start.5) | async-done | bytes 786464 | tf_op jit(solution)/shard_map/all_to_all | solution.py:198
  271.9 2.5 multiply_reduce_fusion
  274.4 1.8 convert_add_fusion
  277.0 10.0 %all_to_all.51 = bf16[4,256,192]{1,2,0:T(8,128)(2,1)S(1)} all-to-all(bf16[4,256,192]{1,2,0:T(8,128)(2,1)S(1)} %bitcast.109), channel_id=1, replica_groups=mesh['dp'=8,'fsdp'=4] {'fsdp'}, dimensions={0} | all-to-all | bytes 786432 | tf_op jit(solution)/shard_map/all_to_all | solution.py:198
  288.3 1.4 copy.178
  289.7 14.7 %attend_back.1 = (bf16[3,64,1024]{2,1,0:T(8,128)(2,1)S(1)}, bf16[3,64,1024]{2,1,0:T(8,128)(2,1)S(1)}, bf16[3,64,1024]{2,1,0:T(8,128)(2,1)S(1)}, f32[3,1,2048]{2,1,0:T(1,128)S(1)}) custom-call(bf16[3,1024,1024]{2,1,0:T(8,128)(2,1)} %get-tuple-element.19.p_ref, bf16[3,1024,64]{2,1,0:T(8,128)(2,1)S(1)} %bitcast.98, ...), custom_call_target="tpu_custom_call" | custom-call | flops 6442450944 | bytes 9437184 | tf_op jit(solution)/shard_map/attend_back/pallas_call | solution.py:160
  304.5 4.0 fusion.18
  308.5 1.2 convolution_convert_fusion.5
  311.9 1.5 convolution_convert_fusion.2
  314.6 1.8 copy.192
  316.3 1.2 pad.24.clone
  317.6 6.9 %convolution_convert_fusion.1 = bf16[3072,768]{1,0:T(8,128)(2,1)} fusion(bf16[512,3072]{1,0:T(8,128)(2,1)} %copy-done.35, bf16[512,896]{1,0:T(8,128)(2,1)} %bitcast.24), kind=kOutput, calls=%fused_computation.11 | convolution fusion | flops 2418278400 | bytes 8650752 | tf_op jit(solution)/shard_map/dot_general | solution.py:41
  325.6 8.3 %convolution_convert_fusion = bf16[3072,768]{1,0:T(8,128)(2,1)} fusion(bf16[512,768]{1,0:T(8,128)(2,1)S(1)} %copy-done.13, f32[512,3072]{1,0:T(8,128)} %copy-done.34), kind=kOutput, calls=%fused_computation.10 | convolution fusion | flops 2432434176 | bytes 11796480 | tf_op jit(solution)/shard_map/dot_general | solution.py:41
  334.0 4.5 all-to-all-start.7
  340.7 1.9 collective-permute-start.1
  342.6 16.1 %collective-permute-done.1 = f32[32,12]{0,1:T(8,128)S(1)} collective-permute-done((f32[32,12]{0,1:T(8,128)S(1)}, f32[32,12]{0,1:T(8,128)S(1)}, u32[]{:S(2)}, u32[]{:S(2)}) %collective-permute-start.1) | collective-permute-done | bytes 1568 | tf_op jit(solution)/shard_map/ppermute | solution.py:206
  359.3 3.1 collective-permute-done.2
  362.5 3.6 collective-permute-done.3
  366.2 1.4 collective-permute-start.4
  367.6 3.1 collective-permute-done.4
  371.3 1.7 convert_reduce_fusion
  373.4 3.3 all-to-all-start.8
  377.7 3.5 all-to-all-done.8
  381.2 58.6 %reduce-scatter.15.cloned.1.call-done = bf16[96,896]{1,0:T(8,128)(2,1)} async-done(((bf16[768,896]{1,0:T(8,128)(2,1)}), bf16[96,896]{1,0:T(8,128)(2,1)}) %reduce-scatter.15.cloned.1.call-update) | async-done | bytes 172048 | tf_op jit(solution)/shard_map/reduce_scatter | solution.py:377
  439.8 3.3 all-to-all-start.9
  446.3 1.9 all-to-all-done.9
  450.2 87.8 %reduce-scatter.9.cloned.1.call-done = bf16[384,768]{1,0:T(8,128)(2,1)} async-done(((bf16[3072,768]{1,0:T(8,128)(2,1)}), bf16[384,768]{1,0:T(8,128)(2,1)}) %reduce-scatter.9.cloned.1.call-update) | async-done | bytes 589840 | tf_op jit(solution)/shard_map/reduce_scatter | solution.py:341
  538.0 1.1 convert_bitcast_fusion
  539.2 1.4 copy.185
  540.5 96.7 %reduce-scatter.11.cloned.1.call-done = bf16[384,768]{1,0:T(8,128)(2,1)} async-done(((bf16[3072,768]{1,0:T(8,128)(2,1)}), bf16[384,768]{1,0:T(8,128)(2,1)}) %reduce-scatter.11.cloned.1.call-update) | async-done | bytes 589840 | tf_op jit(solution)/shard_map/reduce_scatter | solution.py:340
  637.3 2.2 bitcast_convert_fusion
  (174 shorter events, 34.8 us)
Async XLA Ops:
  7.2 22.8 %copy-start = (bf16[32,12]{0,1:T(8,128)(2,1)S(1)}, bf16[32,12]{0,1:T(8,128)(2,1)}, u32[]{:S(2)}) copy-start(bf16[32,12]{0,1:T(8,128)(2,1)} %param.26) | copy-start | bytes 2308
  7.2 19.8 %copy-start.14 = (bf16[1,768,384]{2,1,0:T(8,128)(2,1)S(1)}, bf16[1,768,384]{2,1,0:T(8,128)(2,1)}, u32[]{:S(2)}) copy-start(bf16[1,768,384]{2,1,0:T(8,128)(2,1)} %param.27) | copy-start | bytes 1769476
  7.2 20.0 %copy-start.15 = (bf16[1,384,768]{2,1,0:T(8,128)(2,1)S(1)}, bf16[1,384,768]{2,1,0:T(8,128)(2,1)}, u32[]{:S(2)}) copy-start(bf16[1,384,768]{2,1,0:T(8,128)(2,1)} %param.28) | copy-start | bytes 1769476
  7.2 30.0 %all-gather.5.cloned.1.call-start = ((), (), s32[]{:S(2)}) async-start(), calls=%async_computation.14 | async-start | bytes 1966080 | tf_op jit(solution)/shard_map/all_gather | solution.py:268
  7.9 79.1 %all-gather.7.cloned.1.call-start = ((), (), s32[]{:S(2)}) async-start(), calls=%async_computation.15 | async-start | bytes 2433024 | tf_op jit(solution)/shard_map/all_gather | solution.py:260
  14.0 14.4 %copy-start.16 = (s32[256,1]{0,1:T(1,128)S(1)}, s32[256,1]{0,1:T(1,128)}, u32[]{:S(2)}) copy-start(s32[256,1]{0,1:T(1,128)} %param.18) | copy-start | bytes 3076
  14.0 15.9 %copy-start.26 = (s32[2047]{0:T(1024)S(1)}, s32[2047]{0:T(1024)}, u32[]{:S(2)}) copy-start(s32[2047]{0:T(1024)} %param.17) | copy-start | bytes 24568
  14.0 16.4 %copy-start.32 = (s32[256]{0:T(256)S(1)}, s32[256]{0:T(256)}, u32[]{:S(2)}) copy-start(s32[256]{0:T(256)} %param.16) | copy-start | bytes 3076
  26.9 199.5 %all-gather.9.cloned.1.call-start = ((), (), s32[]{:S(2)}) async-start(), calls=%async_computation.16 | async-start | bytes 10616832 | tf_op jit(solution)/shard_map/all_gather | solution.py:273
  30.0 58.6 %copy-start.27 = (s32[2048]{0:T(1024)}, s32[2048]{0:T(1024)S(1)}, u32[]{:S(2)}) copy-start(s32[2048]{0:T(1024)S(1)} %pad.20) | copy-start | bytes 24580
  39.0 52.5 %copy-start.30 = (f32[1024]{0:T(1024)}, f32[1024]{0:T(1024)S(1)}, u32[]{:S(2)}) copy-start(f32[1024]{0:T(1024)S(1)} %add_rsqrt_fusion) | copy-start | bytes 12292
  93.9 2.0 copy-start.3
  95.9 12.8 %copy-start.2 = (bf16[3,1024,64]{2,1,0:T(8,128)(2,1)}, bf16[3,1024,64]{2,1,0:T(8,128)(2,1)S(1)}, u32[]{:S(2)}) copy-start(bf16[3,1024,64]{2,1,0:T(8,128)(2,1)S(1)} %get-tuple-element.114.v_ref) | copy-start | bytes 1179652
  108.7 4.8 copy-start.22
  108.7 12.2 %copy-start.4 = (bf16[256,768]{1,0:T(8,128)(2,1)S(1)}, bf16[256,768]{1,0:T(8,128)(2,1)}, u32[]{:S(2)}) copy-start(bf16[256,768]{1,0:T(8,128)(2,1)} %param.15) | copy-start | bytes 1179652
  110.0 10.9 %all-to-all-start.1 = ((bf16[4,256,192]{1,2,0:T(8,128)(2,1)}), bf16[4,256,192]{1,2,0:T(8,128)(2,1)S(1)}, u32[]{:S(2)}, u32[]{:S(2)}) async-start(bf16[4,256,192]{1,2,0:T(8,128)(2,1)} %copy.170), calls=%async_computation.1 | async-start | bytes 786432 | tf_op jit(solution)/shard_map/all_to_all | solution.py:198
  120.9 12.0 %copy-start.11 = (bf16[4,256,192]{1,2,0:T(8,128)(2,1)}, bf16[4,256,192]{1,2,0:T(8,128)(2,1)S(1)}, u32[]{:S(2)}) copy-start(bf16[4,256,192]{1,2,0:T(8,128)(2,1)S(1)} %all-to-all-done.1) | copy-start | bytes 1179652
  123.2 0.6 copy-start.23
  123.9 15.2 %copy-start.7 = (bf16[256,768]{1,0:T(8,128)(2,1)}, bf16[256,768]{1,0:T(8,128)(2,1)S(1)}, u32[]{:S(2)}) copy-start(bf16[256,768]{1,0:T(8,128)(2,1)S(1)} %multiply_convert_fusion.1) | copy-start | bytes 1179652
  123.9 13.2 %copy-start.6 = (bf16[256,768]{1,0:T(8,128)(2,1)S(1)}, bf16[256,768]{1,0:T(8,128)(2,1)}, u32[]{:S(2)}) copy-start(bf16[256,768]{1,0:T(8,128)(2,1)} %param.29) | copy-start | bytes 1179652
  125.4 0.5 copy-start.18
  125.9 0.7 copy-start.20
  132.9 17.4 %all-to-all-start.2 = ((bf16[4,128,896]{2,1,0:T(8,128)(2,1)}), bf16[4,128,896]{2,1,0:T(8,128)(2,1)}, u32[]{:S(2)}, u32[]{:S(2)}) async-start(bf16[4,128,896]{2,1,0:T(8,128)(2,1)} %bitcast.114), calls=%async_computation.2 | async-start | bytes 1835008 | tf_op jit(solution)/shard_map/all_to_all | solution.py:198
  150.3 15.3 %all-to-all-start.4 = ((bf16[4,128,768]{2,1,0:T(8,128)(2,1)}), bf16[4,128,768]{2,1,0:T(8,128)(2,1)S(1)}, u32[]{:S(2)}, u32[]{:S(2)}) async-start(bf16[4,128,768]{2,1,0:T(8,128)(2,1)} %bitcast.104), calls=%async_computation.4 | async-start | bytes 1572864 | tf_op jit(solution)/shard_map/all_to_all | solution.py:198
  226.4 5.3 copy-start.33
  231.7 4.6 copy-start.34
  236.3 19.6 %all-to-all-start.3 = ((bf16[4,128,768]{2,1,0:T(8,128)(2,1)}), bf16[4,128,768]{2,1,0:T(8,128)(2,1)S(1)}, u32[]{:S(2)}, u32[]{:S(2)}) async-start(bf16[4,128,768]{2,1,0:T(8,128)(2,1)} %bitcast.116), calls=%async_computation.3 | async-start | bytes 1572864 | tf_op jit(solution)/shard_map/all_to_all | solution.py:198
  248.5 1.7 copy-start.35
  256.0 15.9 %all-to-all-start.5 = ((bf16[4,128,768]{2,1,0:T(8,128)(2,1)}), bf16[4,128,768]{2,1,0:T(8,128)(2,1)}, u32[]{:S(2)}, u32[]{:S(2)}) async-start(bf16[4,128,768]{2,1,0:T(8,128)(2,1)} %bitcast.115), calls=%async_computation.5 | async-start | bytes 1572864 | tf_op jit(solution)/shard_map/all_to_all | solution.py:198
  260.2 113.2 %reduce-scatter.13.cloned.1.call-start = ((), (), s32[]{:S(2)}) async-start(), calls=%async_computation.19 | async-start | bytes 1105920 | tf_op jit(solution)/shard_map/reduce_scatter | solution.py:377
  262.2 0.6 copy-start.24
  271.9 2.5 copy-start.9
  271.9 4.3 copy-start.12
  289.7 14.8 %copy-start.10 = (bf16[1024,768]{1,0:T(8,128)(2,1)S(1)}, bf16[1024,768]{1,0:T(8,128)(2,1)}, u32[]{:S(2)}) copy-start(bf16[1024,768]{1,0:T(8,128)(2,1)} %all-gather.5.cloned.1.call-done) | copy-start | bytes 4718596
  289.7 14.8 %copy-start.31 = (f32[1024]{0:T(1024)S(1)}, f32[1024]{0:T(1024)}, u32[]{:S(2)}) copy-start(f32[1024]{0:T(1024)} %copy-done.30) | copy-start | bytes 12292
  309.8 1.9 copy-start.29
  309.8 1.9 copy-start.8
  309.8 1.9 copy-start.17
  309.8 1.9 copy-start.19
  309.8 1.9 copy-start.21
  309.8 1.9 copy-start.25
  311.6 128.2 %reduce-scatter.15.cloned.1.call-start = ((), (), s32[]{:S(2)}) async-start(), calls=%async_computation.20 | async-start | bytes 1548288 | tf_op jit(solution)/shard_map/reduce_scatter | solution.py:377
  317.6 220.4 %reduce-scatter.9.cloned.1.call-start = ((), (), s32[]{:S(2)}) async-start(), calls=%async_computation.17 | async-start | bytes 5308416 | tf_op jit(solution)/shard_map/reduce_scatter | solution.py:341
  324.5 1.1 copy-start.13
  324.5 312.8 %reduce-scatter.11.cloned.1.call-start = ((), (), s32[]{:S(2)}) async-start(), calls=%async_computation.18 | async-start | bytes 5308416 | tf_op jit(solution)/shard_map/reduce_scatter | solution.py:340
  333.9 4.5 copy-start.28
  333.9 28.4 %copy-start.5 = (bf16[256,768]{1,0:T(8,128)(2,1)S(1)}, bf16[256,768]{1,0:T(8,128)(2,1)}, u32[]{:S(2)}) copy-start(bf16[256,768]{1,0:T(8,128)(2,1)} %param.15) | copy-start | bytes 1179652
  334.0 37.4 %all-to-all-start.7 = ((bf16[4,256,768]{2,1,0:T(8,128)(2,1)}), bf16[4,256,768]{2,1,0:T(8,128)(2,1)}, u32[]{:S(2)}, u32[]{:S(2)}) async-start(bf16[4,256,768]{2,1,0:T(8,128)(2,1)} %bitcast.106), calls=%async_computation.7 | async-start | bytes 3145728 | tf_op jit(solution)/shard_map/all_to_all | solution.py:198
  339.2 1.3 collective-permute-start
  340.7 18.0 %collective-permute-start.1 = (f32[32,12]{0,1:T(8,128)S(1)}, f32[32,12]{0,1:T(8,128)S(1)}, u32[]{:S(2)}, u32[]{:S(2)}) collective-permute-start(f32[32,12]{0,1:T(8,128)S(1)} %add.110), channel_id=1, source_target_pairs={{0,2},{1,3},{2,0},{3,1},{4,6},{5,7},{6,4},{7,5},{8,10},{9,11},{10,... | collective-permute-start | bytes 4616 | tf_op jit(solution)/shard_map/ppermute | solution.py:206
  358.7 3.7 collective-permute-start.2
  362.4 3.8 collective-permute-start.3
  366.2 4.5 collective-permute-start.4
  373.4 7.8 %all-to-all-start.8 = ((bf16[4,24,640]{2,1,0:T(8,128)(2,1)}), bf16[4,24,640]{2,1,0:T(8,128)(2,1)S(1)}, u32[]{:S(2)}, u32[]{:S(2)}) async-start(bf16[4,24,640]{2,1,0:T(8,128)(2,1)} %bitcast.122), calls=%async_computation.8 | async-start | bytes 245760 | tf_op jit(solution)/shard_map/all_to_all | solution.py:198
  439.8 8.4 %all-to-all-start.9 = ((bf16[4,24,896]{2,1,0:T(8,128)(2,1)}), bf16[4,24,896]{2,1,0:T(8,128)(2,1)S(1)}, u32[]{:S(2)}, u32[]{:S(2)}) async-start(bf16[4,24,896]{2,1,0:T(8,128)(2,1)} %bitcast.121), calls=%async_computation.9 | async-start | bytes 344064 | tf_op jit(solution)/shard_map/all_to_all | solution.py:198
  445.6 193.8 %copy-start.1 = (bf16[32,12]{0,1:T(8,128)(2,1)S(1)}, bf16[32,12]{0,1:T(8,128)(2,1)}, u32[]{:S(2)}) copy-start(bf16[32,12]{0,1:T(8,128)(2,1)} %param.26) | copy-start | bytes 2308
Sparse Core Ops, SparseCore 0:
  9.6 24.4 all-gather.4
  36.3 50.6 all-gather.6
  89.8 136.5 all-gather.8
  311.7 60.6 reduce-scatter.12
  376.1 63.6 reduce-scatter.14
  443.7 94.2 reduce-scatter.8
  542.1 95.1 reduce-scatter.10

commit v2 on v1

v2 whole, which is shorter than its diff:
```python
import functools

import jax
import jax.numpy as jnp
from jax import lax
from jax.experimental import pallas as pl
from jax.experimental.pallas import tpu as pltpu
from jax.sharding import PartitionSpec as P

HEADS = 12
HEAD = 64
BUCKETS = 32
LANES = 128
DP = ("z", "y")
EVERY = ("z", "y", "fsdp")
SUBLANES = 8

EPSILON = 1e-06
MASKED = -1000000000.0
HIGHEST = lax.Precision.HIGHEST
BF16 = jnp.bfloat16
F32 = jnp.float32


def inverse_rms(values):
    return lax.rsqrt(jnp.mean(values * values, axis=-1, keepdims=True) + EPSILON)


def norm_gradient(grad, gain, unit, scale):
    inner = grad * gain
    return scale * (inner - unit * jnp.mean(inner * unit, axis=-1, keepdims=True))


def product(left, right):
    return jnp.dot(left, right, preferred_element_type=F32)


def contract(left, left_dim, right, right_dim, precision=None):
    return lax.dot_general(
        left,
        right,
        (((left_dim,), (right_dim,)), ((), ())),
        precision=precision,
        preferred_element_type=F32,
    )


VMEM_LIMIT = 56 * 1024 * 1024


def head_slice(turn, heads, head):
    first = (turn * heads + head) * HEAD
    return slice(first, first + HEAD)


def attend_kernel(
    off_ref, seg_query_ref, seg_key_ref, hidden_ref, weight_ref, *refs, heads, waits
):
    qkv_ref, o_ref, p_ref, skew_ref = refs[waits:]
    turn = pl.program_id(0)
    rows = o_ref.shape[0]
    group = hidden_ref.shape[0]
    width = skew_ref.shape[2]

    @pl.when(turn == 0)
    def _():
        projected = product(hidden_ref[...], weight_ref[:, : 3 * heads * HEAD])
        qkv_ref[...] = projected.astype(BF16)
        for head in range(heads):
            wide = jnp.broadcast_to(off_ref[head : head + 1, :], (LANES, width))
            skew_ref[head] = pltpu.roll(wide, width - (LANES - 1), 1, stride=1, stride_axis=0)

    own_rows = pl.ds(pl.multiple_of(turn * rows, rows), rows)
    for head in range(heads):
        queries = qkv_ref[own_rows, head_slice(0, heads, head)]
        keys = qkv_ref[:, head_slice(1, heads, head)]
        values = qkv_ref[:, head_slice(2, heads, head)]
        scores = contract(queries, 1, keys, 1)
        for part in range(rows // LANES):
            here = slice(part * LANES, (part + 1) * LANES)
            start = group - LANES - turn * rows - part * LANES
            bias = skew_ref[head, :, pl.ds(pl.multiple_of(start, LANES), group)]
            keep = seg_query_ref[here, :] == seg_key_ref[...]
            biased = jnp.where(keep, scores[here] + bias, MASKED)
            top = jnp.max(biased, axis=1, keepdims=True)
            weights = jnp.exp(biased - top)
            total = jnp.sum(weights, axis=1, keepdims=True)
            probs = (weights * (1.0 / total)).astype(BF16)
            p_ref[head, here, :] = probs
            o_ref[here, head_slice(0, heads, head)] = product(probs, values).astype(BF16)


def attend_back_kernel(p_ref, do_ref, qkv_ref, *refs, heads, waits):
    dqkv_ref, doff_ref, dkv_acc, diag = refs[waits:]
    turn = pl.program_id(0)
    rows = do_ref.shape[0]
    group = qkv_ref.shape[0]
    width = diag.shape[2]

    @pl.when(turn == 0)
    def _():
        dkv_acc[...] = jnp.zeros_like(dkv_acc)
        diag[...] = jnp.zeros_like(diag)

    own_rows = pl.ds(pl.multiple_of(turn * rows, rows), rows)
    for head in range(heads):
        queries = qkv_ref[own_rows, head_slice(0, heads, head)]
        keys = qkv_ref[:, head_slice(1, heads, head)]
        values = qkv_ref[:, head_slice(2, heads, head)]
        probs = p_ref[head]
        grad = do_ref[:, head_slice(0, heads, head)]
        grad_probs = contract(grad, 1, values, 1)
        wide = probs.astype(F32)
        correction = jnp.sum(wide * grad_probs, axis=1, keepdims=True)
        grad_scores = (wide * (grad_probs - correction)).astype(BF16)
        dqkv_ref[head_slice(0, heads, head), own_rows] = product(grad_scores, keys).T.astype(BF16)
        dkv_acc[head_slice(0, heads, head), :] += contract(queries, 0, grad_scores, 0)
        dkv_acc[head_slice(1, heads, head), :] += contract(grad, 0, probs, 0)
        for part in range(rows // LANES):
            start = group - LANES - turn * rows - part * LANES
            there = pl.ds(pl.multiple_of(start, LANES), group)
            diag[head, :, there] += grad_scores[part * LANES : (part + 1) * LANES, :].astype(F32)

    @pl.when(turn == pl.num_programs(0) - 1)
    def _():
        dqkv_ref[heads * HEAD :, :] = dkv_acc[...].astype(BF16)
        for head in range(heads):
            lined = jnp.zeros((SUBLANES, width), F32)
            for first in range(0, LANES, SUBLANES):
                lined += pltpu.roll(diag[head, first : first + SUBLANES, :], LANES - 1 - first, 1)
            row = lax.broadcasted_iota(jnp.int32, lined.shape, 0)
            for bit in (1, 2, 4):
                lined = jnp.where((row & bit) != 0, pltpu.roll(lined, width - bit, 1), lined)
            doff_ref[head : head + 1, :] = jnp.sum(lined, axis=0, keepdims=True)


def whole_spec(array):
    return pl.BlockSpec(array.shape, lambda *_: (0,) * array.ndim)


def wait_specs(waits):
    return [pl.BlockSpec(memory_space=pl.ANY)] * len(waits)


def attend(offsets, segment, hidden, dense, waits):
    heads, width = offsets.shape
    group = hidden.shape[0]
    rows = min(256, group)
    own_cols = heads * HEAD
    operands = (offsets, segment[:, None], segment[None, :], hidden, dense)
    specs = [whole_spec(array) for array in operands]
    specs[1] = pl.BlockSpec((rows, 1), lambda b: (b, 0))
    return pl.pallas_call(
        functools.partial(attend_kernel, heads=heads, waits=len(waits)),
        grid=(group // rows,),
        in_specs=specs + wait_specs(waits),
        out_specs=[
            pl.BlockSpec((group, 3 * own_cols), lambda b: (0, 0)),
            pl.BlockSpec((rows, own_cols), lambda b: (b, 0)),
            pl.BlockSpec((heads, rows, group), lambda b: (0, b, 0)),
        ],
        out_shape=[
            jax.ShapeDtypeStruct((group, 3 * own_cols), BF16),
            jax.ShapeDtypeStruct((group, own_cols), BF16),
            jax.ShapeDtypeStruct((heads, group, group), BF16),
        ],
        scratch_shapes=[pltpu.VMEM((heads, LANES, width), F32)],
        compiler_params=pltpu.CompilerParams(vmem_limit_bytes=VMEM_LIMIT),
        cost_estimate=pl.CostEstimate(
            flops=16 * heads * group * group * HEAD,
            bytes_accessed=2 * heads * group * (group + 4 * HEAD),
            transcendentals=heads * group * group,
        ),
        name="attend",
    )(*operands, *waits)


def attend_back(probs, grads, qkv, width, waits):
    heads, group, _ = probs.shape
    rows = min(256, group)
    own_cols = heads * HEAD
    return pl.pallas_call(
        functools.partial(attend_back_kernel, heads=heads, waits=len(waits)),
        grid=(group // rows,),
        in_specs=[
            pl.BlockSpec((heads, rows, group), lambda b: (0, b, 0)),
            pl.BlockSpec((rows, own_cols), lambda b: (b, 0)),
            whole_spec(qkv),
        ]
        + wait_specs(waits),
        out_specs=[
            pl.BlockSpec((3 * own_cols, group), lambda b: (0, 0)),
            pl.BlockSpec((heads, width), lambda b: (0, 0)),
        ],
        out_shape=[
            jax.ShapeDtypeStruct((3 * own_cols, group), BF16),
            jax.ShapeDtypeStruct((heads, width), F32),
        ],
        scratch_shapes=[
            pltpu.VMEM((2 * own_cols, group), F32),
            pltpu.VMEM((heads, LANES, width), F32),
        ],
        compiler_params=pltpu.CompilerParams(vmem_limit_bytes=VMEM_LIMIT),
        cost_estimate=pl.CostEstimate(
            flops=32 * heads * group * group * HEAD,
            bytes_accessed=2 * heads * group * (group + 8 * HEAD),
            transcendentals=0,
        ),
        name="attend_back",
    )(probs, grads, qkv, *waits)


GELU_SLOPE = 0.7978845608028654
GELU_CUBE = 0.044715


def expert_kernel(rows_ref, weights_ref, result_ref, act_ref, slope_ref, acc):
    turn = pl.program_id(0)
    model = rows_ref.shape[1]

    @pl.when(turn == 0)
    def _():
        acc[...] = jnp.zeros_like(acc)

    pre = contract(rows_ref[...], 1, weights_ref[:, :model], 1)
    square = pre * pre
    bend = jnp.tanh(GELU_SLOPE * pre * (1.0 + GELU_CUBE * square))
    half = 0.5 * (1.0 + bend)
    activated = (pre * half).astype(BF16)
    slope = half + 0.5 * GELU_SLOPE * pre * (1.0 - bend * bend) * (1.0 + 3.0 * GELU_CUBE * square)
    act_ref[...] = activated
    slope_ref[...] = slope.astype(BF16)
    acc[...] += product(activated, weights_ref[:, model:])

    @pl.when(turn == pl.num_programs(0) - 1)
    def _():
        result_ref[...] = acc[...].astype(BF16)


def expert_back_kernel(
    rows_ref, grads_ref, weights_ref, act_ref, slope_ref, back_ref, dw_ref, acc
):
    turn = pl.program_id(0)
    model = rows_ref.shape[1]

    @pl.when(turn == 0)
    def _():
        acc[...] = jnp.zeros_like(acc)

    rows, grads = rows_ref[...], grads_ref[...]
    d_act = contract(grads, 1, weights_ref[:, model:], 1)
    d_pre = (slope_ref[...].astype(F32) * d_act).astype(BF16)
    acc[...] += product(d_pre, weights_ref[:, :model])
    dw_ref[:, :model] = contract(d_pre, 0, rows, 0).astype(BF16)
    dw_ref[:, model:] = contract(act_ref[...], 0, grads, 0).astype(BF16)

    @pl.when(turn == pl.num_programs(0) - 1)
    def _():
        back_ref[...] = acc[...].astype(BF16)


def expert_cost(slot_rows, model, units, products):
    return pl.CostEstimate(
        flops=2 * products * slot_rows * model * units,
        bytes_accessed=4 * units * (model + slot_rows),
        transcendentals=0,
    )


def run_expert(rows, weights):
    slot_rows, model = rows.shape
    units, width = weights.shape
    step = min(384, units)
    block = pl.BlockSpec((step, width), lambda i: (i, 0))
    across = pl.BlockSpec((slot_rows, step), lambda i: (0, i))
    hidden = jax.ShapeDtypeStruct((slot_rows, units), BF16)
    return pl.pallas_call(
        expert_kernel,
        grid=(units // step,),
        in_specs=[whole_spec(rows), block],
        out_specs=[whole_spec(rows), across, across],
        out_shape=[jax.ShapeDtypeStruct(rows.shape, BF16), hidden, hidden],
        scratch_shapes=[pltpu.VMEM(rows.shape, F32)],
        compiler_params=pltpu.CompilerParams(vmem_limit_bytes=VMEM_LIMIT),
        cost_estimate=expert_cost(slot_rows, model, units, 2),
        name="run_expert",
    )(rows, weights)


def run_expert_back(rows, grads, weights, activated, slopes):
    slot_rows, model = rows.shape
    units, width = weights.shape
    step = min(384, units)
    block = pl.BlockSpec((step, width), lambda i: (i, 0))
    across = pl.BlockSpec((slot_rows, step), lambda i: (0, i))
    return pl.pallas_call(
        expert_back_kernel,
        grid=(units // step,),
        in_specs=[whole_spec(rows), whole_spec(grads), block, across, across],
        out_specs=[whole_spec(rows), block],
        out_shape=[
            jax.ShapeDtypeStruct(rows.shape, BF16),
            jax.ShapeDtypeStruct((units, width), BF16),
        ],
        scratch_shapes=[pltpu.VMEM(rows.shape, F32)],
        compiler_params=pltpu.CompilerParams(vmem_limit_bytes=VMEM_LIMIT),
        cost_estimate=expert_cost(slot_rows, model, units, 4),
        name="run_expert_back",
    )(rows, grads, weights, activated, slopes)


def exchange(blocks):
    return lax.all_to_all(blocks, "fsdp", split_axis=0, concat_axis=0, tiled=True)


def total_everywhere(part):
    for axis in ("fsdp", "y", "z"):
        size = lax.axis_size(axis)
        step = 1
        while step < size:
            part = part + lax.ppermute(part, axis, [(i, i ^ step) for i in range(size)])
            step *= 2
    return part


def spread(blocks):
    size = lax.axis_size(DP)
    copies = jnp.broadcast_to(blocks[None], (size,) + blocks.shape)
    copies = copies.reshape((size * blocks.shape[0],) + blocks.shape[1:])
    whole = lax.all_to_all(copies, EVERY, split_axis=0, concat_axis=0, tiled=True)
    return whole.reshape((whole.shape[0] * whole.shape[1],) + whole.shape[2:])


def collect(parts):
    size, peers = lax.axis_size(DP), lax.axis_size("fsdp")
    blocks = parts.reshape((size * peers, parts.shape[0] // (size * peers)) + parts.shape[1:])
    blocks = lax.all_to_all(blocks, EVERY, split_axis=0, concat_axis=0, tiled=True)
    return jnp.sum(blocks.reshape((size, peers) + blocks.shape[1:]).astype(F32), axis=0)


def sum_scatter_pairs(blocks, axis):
    size = lax.axis_size(axis)
    if size & (size - 1):
        return jnp.sum(exchange(blocks).astype(F32), axis=0)
    index = lax.axis_index(axis)
    total = lax.dynamic_index_in_dim(blocks, index, 0, keepdims=False).astype(F32)
    for step in range(1, size):
        block = lax.dynamic_index_in_dim(blocks, index ^ step, 0, keepdims=False)
        total += lax.ppermute(block, axis, [(i, i ^ step) for i in range(size)]).astype(F32)
    return total


def zero_of(array):
    first = array[(0,) * array.ndim]
    return (first != first).astype(jnp.int32)


def after(array, other):
    return lax.dynamic_slice_in_dim(array, zero_of(other), array.shape[0], 0)


def gather_pairs(block, axis):
    size = lax.axis_size(axis)
    if size & (size - 1):
        return lax.all_gather(block, axis, axis=0, tiled=True)
    index = lax.axis_index(axis)
    step = 1
    while step < size:
        other = lax.ppermute(block, axis, [(i, i ^ step) for i in range(size)])
        second = (index & step) != 0
        block = jnp.concatenate(
            [jnp.where(second, other, block), jnp.where(second, block, other)], axis=0
        )
        step *= 2
    return block


def pad_lanes(array):
    short = -array.shape[-1] % LANES
    return jnp.pad(array, [(0, 0)] * (array.ndim - 1) + [(0, short)])


def body(
    tokens,
    segment,
    buckets,
    routes,
    w_query,
    w_key,
    w_value,
    w_output,
    w_router,
    norm_attn,
    norm_ffn,
    bias_table,
    expert_in,
    expert_out,
    out_grad,
):
    tok_rows, model = tokens.shape
    shard_rows = w_query.shape[0]
    peers = lax.axis_size("fsdp")
    group = tok_rows * peers
    capacity = 2 * tok_rows // peers
    heads = -(-HEADS // peers)
    own_cols = heads * HEAD
    all_cols = peers * own_cols
    me = lax.axis_index("fsdp")

    def by_peer(matrix):
        padded = jnp.pad(matrix, ((0, 0), (0, all_cols - HEADS * HEAD)))
        return jnp.transpose(padded.reshape(matrix.shape[0], peers, own_cols), (1, 0, 2))

    expert_pack = jnp.concatenate([expert_in[0].T, expert_out[0]], axis=1)

    rest = jnp.concatenate([w_router, norm_attn[:, None], norm_ffn[:, None]], axis=1)
    packed = pad_lanes(
        jnp.concatenate(
            [by_peer(w) for w in (w_query, w_key, w_value, w_output)]
            + [jnp.broadcast_to(rest[None], (peers,) + rest.shape)],
            axis=2,
        )
    )
    dense = spread(packed)
    qkv_cols = 3 * own_cols
    mat_cols = 4 * own_cols
    weight_qkv = dense[:, :qkv_cols]
    weight_router = dense[:, mat_cols : mat_cols + peers]
    gains = dense[:, mat_cols + peers : mat_cols + peers + 2].astype(F32).T
    gain_attn, gain_ffn = gains[0:1], gains[1:2]
    expert_weights = lax.all_gather(after(expert_pack, dense), "z", axis=0, tiled=True)
    output_blocks = gather_pairs(dense[:, qkv_cols:mat_cols], "fsdp").reshape(peers, model, own_cols)
    weight_output = jnp.transpose(output_blocks, (1, 0, 2)).reshape(model, all_cols)[:, :model]

    tokens_all = lax.all_gather(tokens, "fsdp", axis=0, tiled=True)
    segment_all = gather_pairs(segment, "fsdp")

    route = routes[:, 0]
    picked = (route[:, None] == jnp.arange(peers, dtype=jnp.int32)[None, :]).astype(jnp.int32)
    picked_float = picked.astype(F32)
    rank = jnp.sum((jnp.cumsum(picked, axis=0) - 1) * picked, axis=1)
    slot = route * capacity + rank
    slots = peers * capacity
    placing = (jnp.arange(slots, dtype=jnp.int32)[:, None] == slot[None, :]).astype(BF16)

    halves = lax.axis_size("y")

    def place_rows(rows):
        return product(placing, rows).astype(BF16).reshape(peers, capacity, rows.shape[-1])

    def dispatch(rows):
        placed = jnp.concatenate([place_rows(rows)] * halves, axis=0)
        placed = lax.all_to_all(placed, ("y", "fsdp"), split_axis=0, concat_axis=0, tiled=True)
        return placed.reshape(halves * slots, rows.shape[-1])

    def give_back(rows):
        blocks = rows.reshape(halves * peers, capacity, rows.shape[-1])
        blocks = lax.all_to_all(blocks, ("y", "fsdp"), split_axis=0, concat_axis=0, tiled=True)
        blocks = blocks.reshape(halves, slots, rows.shape[-1])
        whole = blocks[0]
        for half in range(1, halves):
            whole = (whole.astype(F32) + blocks[half].astype(F32)).astype(BF16)
        return contract(placing, 0, whole, 0)

    grad_arrived = dispatch(after(out_grad, dense))

    bucket_hot = (
        jnp.pad(buckets, (0, 1), constant_values=-1)[:, None]
        == jnp.arange(BUCKETS, dtype=jnp.int32)[None, :]
    )
    table_pad = jnp.pad(bias_table, ((0, 0), (0, peers * heads - HEADS)))
    own_table = lax.dynamic_slice_in_dim(table_pad, me * heads, heads, 1)
    offsets = contract(own_table, 0, bucket_hot.astype(BF16), 1)

    wide_all = tokens_all.astype(F32)
    unit_all = wide_all * inverse_rms(wide_all)
    hidden = (unit_all * gain_attn).astype(BF16)
    qkv, attended, probs = attend(
        offsets, segment_all, hidden, dense, ()
    )
    blocks = after(attended, grad_arrived).reshape(peers, tok_rows, own_cols)
    attn_out = jnp.transpose(exchange(blocks), (1, 0, 2)).reshape(tok_rows, all_cols)
    attn_out = attn_out[:, : HEADS * HEAD]

    inputs = tokens.astype(F32)
    residual = inputs + product(attn_out, weight_output)
    scale_ffn = inverse_rms(residual)
    unit_ffn = residual * scale_ffn
    hidden2 = (unit_ffn * gain_ffn).astype(BF16)
    logits = product(hidden2, weight_router)
    chances = jax.nn.softmax(logits, axis=-1)
    gate = jnp.sum(chances * picked_float, axis=-1, keepdims=True)

    gate_high = gate.astype(BF16)
    gate_low = (gate - gate_high.astype(F32)).astype(BF16)
    arrived = dispatch(pad_lanes(jnp.concatenate([hidden2, gate_high, gate_low], axis=1)))
    gate_slots = jnp.sum(arrived[:, model : model + 2].astype(F32), axis=1, keepdims=True)
    arrived = arrived[:, :model]
    d_arrived = (gate_slots * grad_arrived.astype(F32)).astype(BF16)
    result, activated, slopes = run_expert(arrived, expert_weights)
    token_result = give_back(result)
    d_rows, d_weights = run_expert_back(arrived, d_arrived, expert_weights, activated, slopes)
    d_expert = lax.psum_scatter(d_weights, "z", scatter_dimension=0, tiled=True).astype(F32)
    d_from_expert = give_back(d_rows)

    mixed = residual + gate * token_result
    grad_out = out_grad.astype(F32)
    d_gate = jnp.sum(grad_out * token_result, axis=-1, keepdims=True)
    d_logits = (gate * (picked_float - chances) * d_gate).astype(BF16)
    d_hidden2 = d_from_expert + contract(d_logits, 1, weight_router, 1)
    d_router = contract(hidden2, 0, d_logits, 0)
    d_gain_ffn = jnp.sum(d_hidden2 * unit_ffn, axis=0)
    d_residual = grad_out + norm_gradient(d_hidden2, gain_ffn, unit_ffn, scale_ffn)
    d_branch = d_residual.astype(BF16)
    d_weight_output = contract(attn_out, 0, d_branch, 0)
    d_attended = contract(d_branch, 1, weight_output, 1).astype(BF16)

    d_heads = exchange(by_peer(d_attended)).reshape(group, own_cols)
    d_qkv, d_offsets = attend_back(probs, d_heads, qkv, offsets.shape[-1], ())
    d_table = contract(bucket_hot.astype(F32), 0, d_offsets, 1, HIGHEST)
    d_table = lax.dynamic_update_slice_in_dim(
        jnp.zeros((BUCKETS, peers * heads), F32), d_table, me * heads, 1
    )
    d_hidden_part = contract(d_qkv, 0, weight_qkv, 1)
    d_gain_attn = jnp.sum(d_hidden_part * unit_all, axis=0)
    d_weight_qkv = contract(hidden, 0, d_qkv, 1)
    d_output_cols = exchange(by_peer(d_weight_output.astype(BF16)))
    d_output_cols = jnp.sum(d_output_cols.astype(F32), axis=0)
    d_rest = jnp.concatenate([d_router, d_gain_attn[:, None], d_gain_ffn[:, None]], axis=1)
    d_dense = jnp.concatenate(
        [
            pad_lanes(d_weight_qkv.astype(BF16)),
            pad_lanes(jnp.concatenate([d_output_cols.astype(BF16), d_rest.astype(BF16)], axis=1)),
        ],
        axis=1,
    )
    d_hidden = sum_scatter_pairs(
        d_hidden_part.astype(BF16).reshape(peers, tok_rows, model), "fsdp"
    )
    scale_attn = inverse_rms(inputs)
    d_inputs = d_residual + norm_gradient(d_hidden, gain_attn, inputs * scale_attn, scale_attn)
    table_total = total_everywhere(d_table)[:, :HEADS]
    d_own = collect(d_dense)
    output_first = qkv_cols + -qkv_cols % LANES
    rest_first = output_first + own_cols
    d_rest = jnp.sum(d_own[:, :, rest_first : rest_first + peers + 2], axis=0)

    def from_peers(first):
        cols = d_own[:, :, first : first + own_cols]
        return jnp.transpose(cols, (1, 0, 2)).reshape(shard_rows, all_cols)[:, : HEADS * HEAD]

    return (
        mixed.astype(BF16),
        d_inputs.astype(BF16),
        from_peers(0),
        from_peers(own_cols),
        from_peers(2 * own_cols),
        from_peers(output_first),
        d_rest[:, :peers],
        d_rest[:, peers],
        d_rest[:, peers + 1],
        table_total,
        d_expert[:, :model].T[None],
        d_expert[:, model:][None],
    )


def solution(mesh):
    dp, fsdp = mesh.shape["dp"], mesh.shape["fsdp"]
    pair = 2 if dp == 8 else 1
    mesh = jax.sharding.Mesh(mesh.devices.reshape(dp // pair, pair, fsdp), ("z", "y", "fsdp"))
    rows = P(("z", "y", "fsdp"), None)
    flat = P(("z", "y", "fsdp"))
    return jax.shard_map(
        body,
        mesh=mesh,
        in_specs=(
            rows,
            flat,
            P(),
            rows,
            rows,
            rows,
            rows,
            rows,
            rows,
            flat,
            flat,
            P(),
            P("fsdp", None, DP),
            P("fsdp", DP, None),
            rows,
        ),
        out_specs=(
            rows,
            rows,
            rows,
            rows,
            rows,
            rows,
            rows,
            flat,
            flat,
            P(),
            P("fsdp", None, DP),
            P("fsdp", DP, None),
        ),
        check_vma=False,
    )
```

time: 655 us -> 331 us (0.51); the launches traced: 647 us -> 330 us
  waiting for transfers between devices: 419 us -> 125 us
  matrix products: 64.4 us -> 17 us
  Pallas kernels: 27.4 us -> 60.1 us
  blocking collectives: 27.9 us -> 0 us
  starting transfers between devices: 35.2 us -> 51.8 us
    reduce_scatter x4 -> x1, waiting for transfers between devices: 243 us -> 0.01 us  [body(): lax.psum_scatter(d_weights, 'z', scatter_dimension=0, tiled=True)]
    all_gather x2 -> x1, waiting for transfers between devices: 107 us -> 0.01 us  [body(): lax.all_gather(after(expert_pack, dense), 'z', axis=0, tiled=True)]
    all_to_all x0 -> x6, waiting for transfers between devices: none -> 67.4 us  [the longest x2 39.2 us: dispatch(): lax.all_to_all(placed, ('y', 'fsdp'), split_axis=0, concat_axis=0, tiled=...]
    pallas_call x2 -> x4, Pallas kernels: 27.4 us -> 60.1 us  [the longest x1 17.1 us: run_expert_back(): pl.pallas_call(expert_back_kernel, grid=(units // step,), in_specs=[whole...]
    all_to_all x8 -> x3, waiting for transfers between devices: 41.1 us -> 8.67 us  [exchange(): lax.all_to_all(blocks, 'fsdp', split_axis=0, concat_axis=0, tiled=True)]
    dot_general x14 -> x10, matrix products: 43 us -> 14.2 us  [contract(): lax.dot_general(left, right, (((left_dim,), (right_dim,)), ((), ())), pre...]
    all_to_all x0 -> x6, starting transfers between devices: none -> 27.8 us  [the longest x2 8.94 us: dispatch(): lax.all_to_all(placed, ('y', 'fsdp'), split_axis=0, concat_axis=0, tiled=...]
    all_to_all x2 -> x0, blocking collectives: 22.8 us -> none  [exchange(): lax.all_to_all(blocks, 'fsdp', split_axis=0, concat_axis=0, tiled=True)]
  transfers between devices with their start and end apart: 20 -> 24, of which waited for: 16 -> 14; matrix products, arithmetic and copies ran while one was open for 14% -> 22% of each run, Pallas kernels for 2% -> 14%
where the time goes in v2:
time: 331 us; the launch traced here: 330 us
  waiting for transfers between devices  125 us (38%)
  Pallas kernels  60.1 us (18%)
  starting transfers between devices  51.8 us (16%)
  local copies, waits for them, and re-layouts  31.9 us (10%)
  other arithmetic  29 us (9%)
  matrix products  17 us (5%)
  between operations  14.6 us (4%)
    all_to_all x2, waiting for transfers between devices, dispatch(): lax.all_to_all(placed, ('y', 'fsdp'), split_axis=0, concat_axis=0, tiled=...  39.2 us
    ppermute x5, waiting for transfers between devices, total_everywhere(): part = part + lax.ppermute(part, axis, [(i, i ^ step) for i in range(size)])  32.6 us
    all_to_all x2, waiting for transfers between devices, give_back(): lax.all_to_all(blocks, ('y', 'fsdp'), split_axis=0, concat_axis=0, tiled=...  20.2 us
    pallas_call x1, Pallas kernels, run_expert_back(): pl.pallas_call(expert_back_kernel, grid=(units // step,), in_specs=[whole...  17.1 us
    pallas_call x1, Pallas kernels, attend(): pl.pallas_call(functools.partial(attend_kernel, heads=heads, waits=len(wa...  14.4 us
    pallas_call x1, Pallas kernels, attend_back(): pl.pallas_call(functools.partial(attend_back_kernel, heads=heads, waits=l...  14.4 us
    dot_general x10, matrix products, contract(): lax.dot_general(left, right, (((left_dim,), (right_dim,)), ((), ())), pre...  14.2 us
    pallas_call x1, Pallas kernels, run_expert(): pl.pallas_call(expert_kernel, grid=(units // step,), in_specs=[whole_spec...  14.2 us
  transfers between devices with their start and end apart: 24, of which 14 were waited for; matrix products, arithmetic and copies ran while one was open for 22% of the time, Pallas kernels for 14%

profile of v2, /device:TPU:0, one launch (start us, length us, event | category | flops | bytes accessed | tf_op | source)
XLA Modules:
  0.0 329.6 jit_solution(7791067524776086025)
XLA Ops:
  12.6 1.2 broadcast_in_dim.29
  13.8 7.3 %all-to-all-start = ((bf16[32,24,896]{2,1,0:T(8,128)(2,1)}), bf16[32,24,896]{2,1,0:T(8,128)(2,1)S(1)}, u32[]{:S(2)}, u32[]{:S(2)}) async-start(bf16[32,24,896]{2,1,0:T(8,128)(2,1)} %bitcast.8), calls=%async_computation | async-start | bytes 2752512 | tf_op jit(solution)/shard_map/all_to_all | solution.py:330
  21.8 2.2 pad_maximum_fusion.3
  24.0 1.2 reduce-window.6
  26.8 1.7 collective-permute-start.1
  29.1 10.5 %collective-permute-done.1 = s32[512]{0:T(512)S(1)} collective-permute-done((s32[512]{0:T(512)S(1)}, s32[512]{0:T(512)S(1)}, u32[]{:S(2)}, u32[]{:S(2)}) %collective-permute-start.1) | collective-permute-done | bytes 2080 | tf_op jit(solution)/shard_map/ppermute | solution.py:369
  39.6 1.1 copy.92.seg_query_ref
  40.7 4.2 %all-gather.3.cloned.1.call-done = bf16[1024,768]{1,0:T(8,128)(2,1)} async-done(((bf16[256,768]{1,0:T(8,128)(2,1)}), bf16[1024,768]{1,0:T(8,128)(2,1)}) %all-gather.3.cloned.1.call-update) | async-done | bytes 1572880 | tf_op jit(solution)/shard_map/all_gather | solution.py:435
  44.9 1.8 fusion.4
  46.7 8.0 %all-to-all-done = bf16[32,24,896]{2,1,0:T(8,128)(2,1)S(1)} async-done(((bf16[32,24,896]{2,1,0:T(8,128)(2,1)}), bf16[32,24,896]{2,1,0:T(8,128)(2,1)S(1)}, u32[]{:S(2)}, u32[]{:S(2)}) %all-to-all-start) | async-done | bytes 1376288 | tf_op jit(solution)/shard_map/all_to_all | solution.py:330
  55.6 1.2 collective-permute-done.2
  58.9 1.1 collective-permute-start.3
  60.0 1.7 fusion.2.hidden_ref
  61.7 14.4 %attend.1 = (bf16[1024,576]{1,0:T(8,128)(2,1)}, bf16[1024,192]{1,0:T(8,128)(2,1)}, bf16[3,1024,1024]{2,1,0:T(8,128)(2,1)}) custom-call(f32[3,2048]{1,0:T(4,128)} %fusion.9.off_ref, s32[1024,1]{1,0:T(8,128)} %copy.92.seg_query_ref, s32[1,1024]{1,0:T(1,128)} %bitcast.145, bf16[1024,768]{1,0:T(8,128)(2,1)} %fusion.2.hidden_ref, bf16[768,896]{1,0:T(8,128)(2,1)} %bitcast.110), custom_call_target="tpu_custom_call" | custom-call | flops 3221225472 | bytes 7864320 | tf_op jit(solution)/shard_map/attend/pallas_call | solution.py:153
  76.1 2.0 copy.93
  78.1 3.5 %all-to-all-start.1 = ((bf16[4,256,192]{1,2,0:T(8,128)(2,1)}), bf16[4,256,192]{1,2,0:T(8,128)(2,1)S(1)}, u32[]{:S(2)}, u32[]{:S(2)}) async-start(bf16[4,256,192]{1,2,0:T(8,128)(2,1)} %copy.93), calls=%async_computation.1 | async-start | bytes 786432 | tf_op jit(solution)/shard_map/all_to_all | solution.py:313
  82.2 1.4 pad_maximum_fusion.1
  83.6 1.7 copy.97
  85.4 3.6 %all-to-all-done.1 = bf16[4,256,192]{1,2,0:T(8,128)(2,1)S(1)} async-done(((bf16[4,256,192]{1,2,0:T(8,128)(2,1)}), bf16[4,256,192]{1,2,0:T(8,128)(2,1)S(1)}, u32[]{:S(2)}, u32[]{:S(2)}) %all-to-all-start.1) | async-done | bytes 393248 | tf_op jit(solution)/shard_map/all_to_all | solution.py:313
  90.3 1.3 fusion.64
  93.1 1.4 pad_maximum_fusion
  94.5 4.5 %all-to-all-start.2 = ((bf16[8,128,896]{2,1,0:T(8,128)(2,1)}), bf16[8,128,896]{2,1,0:T(8,128)(2,1)}, u32[]{:S(2)}, u32[]{:S(2)}) async-start(bf16[8,128,896]{2,1,0:T(8,128)(2,1)} %pad_maximum_fusion), calls=%async_computation.2 | async-start | bytes 3670016 | tf_op jit(solution)/shard_map/all_to_all | solution.py:453
  99.3 1.3 pad_maximum_fusion.2
  100.7 22.1 %all-to-all-done.2 = bf16[8,128,896]{2,1,0:T(8,128)(2,1)} async-done(((bf16[8,128,896]{2,1,0:T(8,128)(2,1)}), bf16[8,128,896]{2,1,0:T(8,128)(2,1)}, u32[]{:S(2)}, u32[]{:S(2)}) %all-to-all-start.2) | async-done | bytes 1835040 | tf_op jit(solution)/shard_map/all_to_all | solution.py:453
  122.8 4.5 %all-to-all-start.4 = ((bf16[8,128,768]{2,1,0:T(8,128)(2,1)}), bf16[8,128,768]{2,1,0:T(8,128)(2,1)}, u32[]{:S(2)}, u32[]{:S(2)}) async-start(bf16[8,128,768]{2,1,0:T(8,128)(2,1)} %pad_maximum_fusion.2), calls=%async_computation.4 | async-start | bytes 3145728 | tf_op jit(solution)/shard_map/all_to_all | solution.py:453
  127.3 2.7 slice.109.rows_ref
  130.0 1.1 convert_reduce_fusion.1
  131.1 17.1 %all-to-all-done.4 = bf16[8,128,768]{2,1,0:T(8,128)(2,1)} async-done(((bf16[8,128,768]{2,1,0:T(8,128)(2,1)}), bf16[8,128,768]{2,1,0:T(8,128)(2,1)}, u32[]{:S(2)}, u32[]{:S(2)}) %all-to-all-start.4) | async-done | bytes 1572896 | tf_op jit(solution)/shard_map/all_to_all | solution.py:453
  148.1 2.9 fusion.5.grads_ref
  151.0 14.2 %run_expert.1 = (bf16[1024,768]{1,0:T(8,128)(2,1)}, bf16[1024,1536]{1,0:T(8,128)(2,1)}, bf16[1024,1536]{1,0:T(8,128)(2,1)}) custom-call(bf16[1024,768]{1,0:T(8,128)(2,1)} %slice.109.rows_ref, bf16[1536,1536]{1,0:T(8,128)(2,1)} %all-gather.5.cloned.1.call-done.weights_ref), custom_call_target="tpu_custom_call" | custom-call | flops 4831838208 | bytes 11010048 | tf_op jit(solution)/shard_map/run_expert/pallas_call | solution.py:277
  165.2 4.3 %all-to-all-start.3 = ((bf16[8,128,768]{2,1,0:T(8,128)(2,1)}), bf16[8,128,768]{2,1,0:T(8,128)(2,1)}, u32[]{:S(2)}, u32[]{:S(2)}) async-start(bf16[8,128,768]{2,1,0:T(8,128)(2,1)} %bitcast.126), calls=%async_computation.3 | async-start | bytes 3145728 | tf_op jit(solution)/shard_map/all_to_all | solution.py:458
  169.6 17.1 %run_expert_back.1 = (bf16[1024,768]{1,0:T(8,128)(2,1)}, bf16[1536,1536]{1,0:T(8,128)(2,1)}) custom-call(bf16[1024,768]{1,0:T(8,128)(2,1)} %slice.109.rows_ref, bf16[1024,768]{1,0:T(8,128)(2,1)} %fusion.5.grads_ref, bf16[1536,1536]{1,0:T(8,128)(2,1)} %all-gather.5.cloned.1.call-done.weights_ref, bf16[1024,1536]{1,0:T(8,128)(2,1)} %get-tuple-element.24.act_ref, ...), custom_call_target="tpu_custom_call" | custom-call | flops 9663676416 | bytes 11010048 | tf_op jit(solution)/shard_map/run_expert_back/pallas_call | solution.py:296
  186.7 3.9 %all-to-all-done.3 = bf16[8,128,768]{2,1,0:T(8,128)(2,1)} async-done(((bf16[8,128,768]{2,1,0:T(8,128)(2,1)}), bf16[8,128,768]{2,1,0:T(8,128)(2,1)}, u32[]{:S(2)}, u32[]{:S(2)}) %all-to-all-start.3) | async-done | bytes 1572896 | tf_op jit(solution)/shard_map/all_to_all | solution.py:458
  190.6 4.4 %all-to-all-start.5 = ((bf16[8,128,768]{2,1,0:T(8,128)(2,1)}), bf16[8,128,768]{2,1,0:T(8,128)(2,1)}, u32[]{:S(2)}, u32[]{:S(2)}) async-start(bf16[8,128,768]{2,1,0:T(8,128)(2,1)} %bitcast.125), calls=%async_computation.5 | async-start | bytes 3145728 | tf_op jit(solution)/shard_map/all_to_all | solution.py:458
  195.0 1.6 add_convert_fusion.1
  196.6 1.3 fusion.22
  198.4 1.3 fusion.53
  199.7 16.3 %all-to-all-done.5 = bf16[8,128,768]{2,1,0:T(8,128)(2,1)} async-done(((bf16[8,128,768]{2,1,0:T(8,128)(2,1)}), bf16[8,128,768]{2,1,0:T(8,128)(2,1)}, u32[]{:S(2)}, u32[]{:S(2)}) %all-to-all-start.5) | async-done | bytes 1572896 | tf_op jit(solution)/shard_map/all_to_all | solution.py:458
  216.0 1.6 add_convert_fusion
  217.6 2.0 multiply_reduce_fusion
  219.6 1.1 convert_add_fusion
  222.1 3.5 %all-to-all-start.6 = ((bf16[4,256,192]{1,2,0:T(8,128)(2,1)}), bf16[4,256,192]{1,2,0:T(8,128)(2,1)S(1)}, u32[]{:S(2)}, u32[]{:S(2)}) async-start(bf16[4,256,192]{1,2,0:T(8,128)(2,1)} %bitcast.35), calls=%async_computation.6 | async-start | bytes 786432 | tf_op jit(solution)/shard_map/all_to_all | solution.py:313
  226.4 1.5 convolution_convert_fusion
  227.9 5.0 %all-to-all-done.6 = bf16[4,256,192]{1,2,0:T(8,128)(2,1)S(1)} async-done(((bf16[4,256,192]{1,2,0:T(8,128)(2,1)}), bf16[4,256,192]{1,2,0:T(8,128)(2,1)S(1)}, u32[]{:S(2)}, u32[]{:S(2)}) %all-to-all-start.6) | async-done | bytes 393248 | tf_op jit(solution)/shard_map/all_to_all | solution.py:313
  233.0 3.8 %all-to-all-start.7 = ((bf16[4,768,192]{1,2,0:T(8,128)(2,1)}), bf16[4,768,192]{1,2,0:T(8,128)(2,1)S(1)}, u32[]{:S(2)}, u32[]{:S(2)}) async-start(bf16[4,768,192]{1,2,0:T(8,128)(2,1)} %bitcast.44), calls=%async_computation.7 | async-start | bytes 2359296 | tf_op jit(solution)/shard_map/all_to_all | solution.py:313
  237.8 14.4 %attend_back.1 = (bf16[576,1024]{1,0:T(8,128)(2,1)}, f32[3,2048]{1,0:T(4,128)}) custom-call(bf16[3,1024,1024]{2,1,0:T(8,128)(2,1)} %get-tuple-element.27.p_ref, bf16[1024,192]{1,0:T(8,128)(2,1)} %bitcast.130, bf16[1024,576]{1,0:T(8,128)(2,1)} %get-tuple-element.28.qkv_ref), custom_call_target="tpu_custom_call" | custom-call | flops 6442450944 | bytes 9437184 | tf_op jit(solution)/shard_map/attend_back/pallas_call | solution.py:182
  252.2 4.2 %fusion.3 = (bf16[768]{0:T(1024)(128)(2,1)S(1)}, bf16[1024,768]{1,0:T(8,128)(2,1)}) fusion(bf16[1024,768]{1,0:T(8,128)(2,1)S(1)} %copy-done.4, f32[1024]{0:T(1024)S(1)} %copy-done.25, bf16[576,1024]{1,0:T(8,128)(2,1)} %get-tuple-element.29, bf16[768,896]{1,0:T(8,128)(2,1)S(1)} %bitcast.113), kind=kOutput, calls=%fused_computation.5 | convolution fusion | flops 909901056 | bytes 5314048 | tf_op jit(solution)/shard_map/dot_general | solution.py:39
  257.0 1.1 convolution_convert_fusion.2
  259.2 1.6 copy.105
  260.8 2.9 all-to-all-start.8
  264.8 2.3 dynamic-slice_bitcast_fusion.2
  267.4 1.8 collective-permute-start.5
  269.3 1.6 collective-permute-start.8
  270.9 26.6 %collective-permute-done.8 = f32[32,12]{0,1:T(8,128)S(1)} collective-permute-done((f32[32,12]{0,1:T(8,128)S(1)}, f32[32,12]{0,1:T(8,128)S(1)}, u32[]{:S(2)}, u32[]{:S(2)}) %collective-permute-start.8) | collective-permute-done | bytes 1568 | tf_op jit(solution)/shard_map/ppermute | solution.py:321
  297.5 2.2 collective-permute-start.9
  299.7 1.6 collective-permute-done.9
  302.3 2.7 collective-permute-done.10
  305.0 3.1 collective-permute-start.11
  308.1 1.6 collective-permute-done.11
  310.3 1.5 fusion.17
  311.9 2.3 fusion.21
  319.0 1.5 convert_element_type.214
  320.5 1.2 slice_bitcast_fusion
  321.7 1.4 copy.112
  (187 shorter events, 28.0 us)
Async XLA Ops:
  7.2 18.5 %copy-start = (bf16[32,12]{0,1:T(8,128)(2,1)S(1)}, bf16[32,12]{0,1:T(8,128)(2,1)}, u32[]{:S(2)}) copy-start(bf16[32,12]{0,1:T(8,128)(2,1)} %param.26) | copy-start | bytes 2308
  7.2 37.7 %all-gather.3.cloned.1.call-start = ((), (), s32[]{:S(2)}) async-start(), calls=%async_computation.10 | async-start | bytes 1966080 | tf_op jit(solution)/shard_map/all_gather | solution.py:435
  13.8 7.4 %copy-start.39 = (s32[256]{0:T(256)S(1)}, s32[256]{0:T(256)}, u32[]{:S(2)}) copy-start(s32[256]{0:T(256)} %param.16) | copy-start | bytes 3076
  13.8 7.7 %copy-start.15 = (bf16[1,768,384]{2,1,0:T(8,128)(2,1)S(1)}, bf16[1,768,384]{2,1,0:T(8,128)(2,1)}, u32[]{:S(2)}) copy-start(bf16[1,768,384]{2,1,0:T(8,128)(2,1)} %param.27) | copy-start | bytes 1769476
  13.8 40.9 %all-to-all-start = ((bf16[32,24,896]{2,1,0:T(8,128)(2,1)}), bf16[32,24,896]{2,1,0:T(8,128)(2,1)S(1)}, u32[]{:S(2)}, u32[]{:S(2)}) async-start(bf16[32,24,896]{2,1,0:T(8,128)(2,1)} %bitcast.8), calls=%async_computation | async-start | bytes 2752512 | tf_op jit(solution)/shard_map/all_to_all | solution.py:330
  21.1 129.9 %all-gather.5.cloned.1.call-start = ((), (), s32[]{:S(2)}) async-start(), calls=%async_computation.11 | async-start | bytes 5898240 | tf_op jit(solution)/shard_map/all_gather | solution.py:431
  21.2 5.6 %collective-permute-start = (s32[256]{0:T(256)S(1)}, s32[256]{0:T(256)S(1)}, u32[]{:S(2)}, u32[]{:S(2)}) collective-permute-start(s32[256]{0:T(256)S(1)} %copy-done.39), channel_id=1, source_target_pairs={{0,1},{1,0},{2,3},{3,2},{4,5},{5,4},{6,7},{7,6},{8,9},{9,8},{10,11... | collective-permute-start | bytes 3080 | tf_op jit(solution)/shard_map/ppermute | solution.py:369
  21.8 2.2 copy-start.16
  21.8 3.8 %copy-start.35 = (s32[2047]{0:T(1024)S(1)}, s32[2047]{0:T(1024)}, u32[]{:S(2)}) copy-start(s32[2047]{0:T(1024)} %param.17) | copy-start | bytes 24568
  25.6 29.4 %copy-start.36 = (s32[2048]{0:T(1024)}, s32[2048]{0:T(1024)S(1)}, u32[]{:S(2)}) copy-start(s32[2048]{0:T(1024)S(1)} %pad.20) | copy-start | bytes 24580
  26.8 12.8 %collective-permute-start.1 = (s32[512]{0:T(512)S(1)}, s32[512]{0:T(512)S(1)}, u32[]{:S(2)}, u32[]{:S(2)}) collective-permute-start(s32[512]{0:T(512)S(1)} %pad_add_fusion.1), channel_id=1, source_target_pairs={{0,2},{1,3},{2,0},{3,1},{4,6},{5,7},{6,4},{7,5},{8,10},{9,11},{10,... | collective-permute-start | bytes 6152 | tf_op jit(solution)/shard_map/ppermute | solution.py:369
  39.6 15.5 %copy-start.26 = (s32[1024]{0:T(1024)}, s32[1024]{0:T(1024)S(1)}, u32[]{:S(2)}) copy-start(s32[1024]{0:T(1024)S(1)} %pad_add_fusion) | copy-start | bytes 12292
  46.7 13.3 %copy-start.24 = (f32[1024]{0:T(1024)}, f32[1024]{0:T(1024)S(1)}, u32[]{:S(2)}) copy-start(f32[1024]{0:T(1024)S(1)} %add_rsqrt_fusion) | copy-start | bytes 12292
  54.8 2.2 copy-start.5
  55.0 1.8 collective-permute-start.2
  56.9 0.7 copy-start.11
  57.0 3.0 copy-start.3
  58.9 22.7 %collective-permute-start.3 = (bf16[1536,192]{0,1:T(8,128)(2,1)}, bf16[1536,192]{0,1:T(8,128)(2,1)S(1)}, u32[]{:S(2)}, u32[]{:S(2)}) collective-permute-start(bf16[1536,192]{0,1:T(8,128)(2,1)} %copy.94), channel_id=1, source_target_pairs={{0,2},{1,3},{2,0},{3,1},{4,6},{5,7},{6,4},{7,5},{8,10},{9,11},{10,... | collective-permute-start | bytes 1769480 | tf_op jit(solution)/shard_map/ppermute | solution.py:369
  76.1 5.8 %copy-start.12 = (bf16[768,192]{1,0:T(8,128)(2,1)S(1)}, bf16[768,192]{1,0:T(8,128)(2,1)}, u32[]{:S(2)}) copy-start(bf16[768,192]{1,0:T(8,128)(2,1)} %copy-done.11) | copy-start | bytes 884740
  78.1 10.9 %all-to-all-start.1 = ((bf16[4,256,192]{1,2,0:T(8,128)(2,1)}), bf16[4,256,192]{1,2,0:T(8,128)(2,1)S(1)}, u32[]{:S(2)}, u32[]{:S(2)}) async-start(bf16[4,256,192]{1,2,0:T(8,128)(2,1)} %copy.93), calls=%async_computation.1 | async-start | bytes 786432 | tf_op jit(solution)/shard_map/all_to_all | solution.py:313
  83.6 5.4 %copy-start.2 = (bf16[256,768]{1,0:T(8,128)(2,1)S(1)}, bf16[256,768]{1,0:T(8,128)(2,1)}, u32[]{:S(2)}) copy-start(bf16[256,768]{1,0:T(8,128)(2,1)} %param.15) | copy-start | bytes 1179652
  89.6 2.1 copy-start.17
  89.6 3.0 copy-start.30
  90.3 2.7 copy-start.9
  91.7 0.6 copy-start.20
  94.5 4.5 %copy-start.7 = (bf16[256,768]{1,0:T(8,128)(2,1)S(1)}, bf16[256,768]{1,0:T(8,128)(2,1)}, u32[]{:S(2)}) copy-start(bf16[256,768]{1,0:T(8,128)(2,1)} %param.29) | copy-start | bytes 1179652
  94.5 28.3 %all-to-all-start.2 = ((bf16[8,128,896]{2,1,0:T(8,128)(2,1)}), bf16[8,128,896]{2,1,0:T(8,128)(2,1)}, u32[]{:S(2)}, u32[]{:S(2)}) async-start(bf16[8,128,896]{2,1,0:T(8,128)(2,1)} %pad_maximum_fusion), calls=%async_computation.2 | async-start | bytes 3670016 | tf_op jit(solution)/shard_map/all_to_all | solution.py:453
  122.8 25.3 %all-to-all-start.4 = ((bf16[8,128,768]{2,1,0:T(8,128)(2,1)}), bf16[8,128,768]{2,1,0:T(8,128)(2,1)}, u32[]{:S(2)}, u32[]{:S(2)}) async-start(bf16[8,128,768]{2,1,0:T(8,128)(2,1)} %pad_maximum_fusion.2), calls=%async_computation.4 | async-start | bytes 3145728 | tf_op jit(solution)/shard_map/all_to_all | solution.py:453
  165.2 25.3 %all-to-all-start.3 = ((bf16[8,128,768]{2,1,0:T(8,128)(2,1)}), bf16[8,128,768]{2,1,0:T(8,128)(2,1)}, u32[]{:S(2)}, u32[]{:S(2)}) async-start(bf16[8,128,768]{2,1,0:T(8,128)(2,1)} %bitcast.126), calls=%async_computation.3 | async-start | bytes 3145728 | tf_op jit(solution)/shard_map/all_to_all | solution.py:458
  169.5 149.4 %reduce-scatter.2.cloned.1.call-start = ((), (), s32[]{:S(2)}) async-start(), calls=%async_computation.12 | async-start | bytes 5898240 | tf_op jit(solution)/shard_map/reduce_scatter | solution.py:503
  190.6 25.4 %all-to-all-start.5 = ((bf16[8,128,768]{2,1,0:T(8,128)(2,1)}), bf16[8,128,768]{2,1,0:T(8,128)(2,1)}, u32[]{:S(2)}, u32[]{:S(2)}) async-start(bf16[8,128,768]{2,1,0:T(8,128)(2,1)} %bitcast.125), calls=%async_computation.5 | async-start | bytes 3145728 | tf_op jit(solution)/shard_map/all_to_all | solution.py:458
  196.5 1.9 copy-start.18
  196.5 1.9 copy-start.21
  196.5 1.9 copy-start.28
  197.9 0.6 copy-start.33
  217.6 2.0 copy-start.8
  217.6 2.0 copy-start.13
  217.6 2.0 copy-start.32
  220.7 4.9 %copy-start.10 = (bf16[256,768]{1,0:T(8,128)(2,1)S(1)}, bf16[256,768]{1,0:T(8,128)(2,1)}, u32[]{:S(2)}) copy-start(bf16[256,768]{1,0:T(8,128)(2,1)} %copy-done.9) | copy-start | bytes 1179652
  220.7 4.9 %copy-start.19 = (s32[256,1]{0,1:T(1,128)S(1)}, s32[256,1]{0,1:T(1,128)}, u32[]{:S(2)}) copy-start(s32[256,1]{0,1:T(1,128)} %param.18) | copy-start | bytes 3076
  221.1 4.5 %copy-start.22 = (f32[256]{0:T(256)S(1)}, f32[256]{0:T(256)}, u32[]{:S(2)}) copy-start(f32[256]{0:T(256)} %copy-done.20) | copy-start | bytes 3076
  221.1 4.5 %copy-start.29 = (f32[256]{0:T(256)S(1)}, f32[256]{0:T(256)}, u32[]{:S(2)}) copy-start(f32[256]{0:T(256)} %copy-done.27) | copy-start | bytes 3076
  221.2 4.5 %copy-start.34 = (f32[256]{0:T(256)S(1)}, f32[256]{0:T(256)}, u32[]{:S(2)}) copy-start(f32[256]{0:T(256)} %copy-done.33) | copy-start | bytes 3076
  221.2 5.2 %copy-start.38 = (bf16[768]{0:T(1024)(128)(2,1)S(1)}, bf16[768]{0:T(1024)(128)(2,1)}, u32[]{:S(2)}) copy-start(bf16[768]{0:T(1024)(128)(2,1)} %get-tuple-element.92) | copy-start | bytes 4612
  222.1 10.9 %all-to-all-start.6 = ((bf16[4,256,192]{1,2,0:T(8,128)(2,1)}), bf16[4,256,192]{1,2,0:T(8,128)(2,1)S(1)}, u32[]{:S(2)}, u32[]{:S(2)}) async-start(bf16[4,256,192]{1,2,0:T(8,128)(2,1)} %bitcast.35), calls=%async_computation.6 | async-start | bytes 786432 | tf_op jit(solution)/shard_map/all_to_all | solution.py:313
  233.0 25.1 %all-to-all-start.7 = ((bf16[4,768,192]{1,2,0:T(8,128)(2,1)}), bf16[4,768,192]{1,2,0:T(8,128)(2,1)S(1)}, u32[]{:S(2)}, u32[]{:S(2)}) async-start(bf16[4,768,192]{1,2,0:T(8,128)(2,1)} %bitcast.44), calls=%async_computation.7 | async-start | bytes 2359296 | tf_op jit(solution)/shard_map/all_to_all | solution.py:313
  237.8 14.4 %copy-start.4 = (bf16[1024,768]{1,0:T(8,128)(2,1)S(1)}, bf16[1024,768]{1,0:T(8,128)(2,1)}, u32[]{:S(2)}) copy-start(bf16[1024,768]{1,0:T(8,128)(2,1)} %all-gather.3.cloned.1.call-done) | copy-start | bytes 4718596
  237.8 14.4 %copy-start.6 = (bf16[32,24,896]{2,1,0:T(8,128)(2,1)S(1)}, bf16[32,24,896]{2,1,0:T(8,128)(2,1)}, u32[]{:S(2)}) copy-start(bf16[32,24,896]{2,1,0:T(8,128)(2,1)} %copy-done.5) | copy-start | bytes 4128772
  237.8 14.4 %copy-start.25 = (f32[1024]{0:T(1024)S(1)}, f32[1024]{0:T(1024)}, u32[]{:S(2)}) copy-start(f32[1024]{0:T(1024)} %copy-done.24) | copy-start | bytes 12292
  252.2 4.8 %copy-start.14 = (bf16[1024,768]{1,0:T(8,128)(2,1)S(1)}, bf16[1024,768]{1,0:T(8,128)(2,1)}, u32[]{:S(2)}) copy-start(bf16[1024,768]{1,0:T(8,128)(2,1)} %fusion.2.hidden_ref) | copy-start | bytes 4718596
  252.2 4.8 %copy-start.41 = (bf16[576,1024]{1,0:T(8,128)(2,1)S(1)}, bf16[576,1024]{1,0:T(8,128)(2,1)}, u32[]{:S(2)}) copy-start(bf16[576,1024]{1,0:T(8,128)(2,1)} %get-tuple-element.29) | copy-start | bytes 3538948
  257.0 1.4 copy-start.23
  260.8 3.0 copy-start.37
  260.8 3.0 copy-start.40
  260.8 53.3 %all-to-all-start.8 = ((bf16[32,24,896]{2,1,0:T(8,128)(2,1)}), bf16[32,24,896]{2,1,0:T(8,128)(2,1)S(1)}, u32[]{:S(2)}, u32[]{:S(2)}) async-start(bf16[32,24,896]{2,1,0:T(8,128)(2,1)} %bitcast.115), calls=%async_computation.8 | async-start | bytes 2752512 | tf_op jit(solution)/shard_map/all_to_all | solution.py:337
  264.5 4.6 %collective-permute-start.7 = (f32[32,12]{0,1:T(8,128)S(1)}, f32[32,12]{0,1:T(8,128)S(1)}, u32[]{:S(2)}, u32[]{:S(2)}) collective-permute-start(f32[32,12]{0,1:T(8,128)S(1)} %dynamic_update_slice.5), channel_id=1, source_target_pairs={{0,1},{1,0},{2,3},{3,2},{4,5},{5,4},{6,7},{7,6},{8,9},{9,8},{10,11... | collective-permute-start | bytes 4616 | tf_op jit(solution)/shard_map/ppermute | solution.py:321
  267.1 43.2 %collective-permute-start.4 = (bf16[256,768]{1,0:T(8,128)(2,1)}, bf16[256,768]{1,0:T(8,128)(2,1)S(1)}, u32[]{:S(2)}, u32[]{:S(2)}) collective-permute-start(bf16[256,768]{1,0:T(8,128)(2,1)} %get-tuple-element.104), channel_id=1, source_target_pairs={{0,1},{1,0},{2,3},{3,2},{4,5},{5,4},{6,7},{7,6},{8,9},{9,8},{10,11... | collective-permute-start | bytes 1179656 | tf_op jit(solution)/shard_map/ppermute | solution.py:349
  267.4 43.0 %collective-permute-start.5 = (bf16[256,768]{1,0:T(8,128)(2,1)}, bf16[256,768]{1,0:T(8,128)(2,1)S(1)}, u32[]{:S(2)}, u32[]{:S(2)}) collective-permute-start(bf16[256,768]{1,0:T(8,128)(2,1)} %get-tuple-element.106), channel_id=1, source_target_pairs={{0,2},{1,3},{2,0},{3,1},{4,6},{5,7},{6,4},{7,5},{8,10},{9,11},{10,... | collective-permute-start | bytes 1179656 | tf_op jit(solution)/shard_map/ppermute | solution.py:349
  269.1 41.2 %collective-permute-start.6 = (bf16[256,768]{1,0:T(8,128)(2,1)}, bf16[256,768]{1,0:T(8,128)(2,1)}, u32[]{:S(2)}, u32[]{:S(2)}) collective-permute-start(bf16[256,768]{1,0:T(8,128)(2,1)} %get-tuple-element.105), channel_id=1, source_target_pairs={{0,3},{1,2},{2,1},{3,0},{4,7},{5,6},{6,5},{7,4},{8,11},{9,10},{10,... | collective-permute-start | bytes 1179656 | tf_op jit(solution)/shard_map/ppermute | solution.py:349
  269.3 28.2 %collective-permute-start.8 = (f32[32,12]{0,1:T(8,128)S(1)}, f32[32,12]{0,1:T(8,128)S(1)}, u32[]{:S(2)}, u32[]{:S(2)}) collective-permute-start(f32[32,12]{0,1:T(8,128)S(1)} %add.137), channel_id=1, source_target_pairs={{0,2},{1,3},{2,0},{3,1},{4,6},{5,7},{6,4},{7,5},{8,10},{9,11},{10,... | collective-permute-start | bytes 4616 | tf_op jit(solution)/shard_map/ppermute | solution.py:321
  297.5 3.9 %collective-permute-start.9 = (f32[32,12]{0,1:T(8,128)S(1)}, f32[32,12]{0,1:T(8,128)S(1)}, u32[]{:S(2)}, u32[]{:S(2)}) collective-permute-start(f32[32,12]{0,1:T(8,128)S(1)} %add.138), channel_id=1, source_target_pairs={{0,4},{4,0},{1,5},{5,1},{2,6},{6,2},{3,7},{7,3},{8,12},{12,8},{9,1... | collective-permute-start | bytes 4616 | tf_op jit(solution)/shard_map/ppermute | solution.py:321
  301.4 3.7 %collective-permute-start.10 = (f32[32,12]{0,1:T(8,128)S(1)}, f32[32,12]{0,1:T(8,128)S(1)}, u32[]{:S(2)}, u32[]{:S(2)}) collective-permute-start(f32[32,12]{0,1:T(8,128)S(1)} %add.139), channel_id=1, source_target_pairs={{0,8},{8,0},{16,24},{24,16},{1,9},{9,1},{17,25},{25,17},{2,10},{10... | collective-permute-start | bytes 4616 | tf_op jit(solution)/shard_map/ppermute | solution.py:321
  305.0 4.7 %collective-permute-start.11 = (f32[32,12]{0,1:T(8,128)S(1)}, f32[32,12]{0,1:T(8,128)S(1)}, u32[]{:S(2)}, u32[]{:S(2)}) collective-permute-start(f32[32,12]{0,1:T(8,128)S(1)} %add.140), channel_id=1, source_target_pairs={{0,16},{8,24},{16,0},{24,8},{1,17},{9,25},{17,1},{25,9},{2,18},{10... | collective-permute-start | bytes 4616 | tf_op jit(solution)/shard_map/ppermute | solution.py:321
  320.5 2.6 copy-start.1
  (2 other events, 1.1 us)
Sparse Core Ops, SparseCore 0:
  9.6 35.2 all-gather.2
  47.1 89.0 all-gather.4
  186.8 86.7 reduce-scatter.1
